TPU v7x, 256 devices: a whole 4x4x8 slice. The times are simulated.
256 devices in a mesh: expert: 128 (over z, y, x), dp: 2 (over core).
Axes of the slice: x: 4, y: 4, z: 8, core: 2. Of those that a mesh axis runs over, the one named last changes fastest.
Arguments:
- tokens: bfloat16 [2, 16384, 2048], P('dp', 'expert'), may hold values from -6 to 6
- grad_out: bfloat16 [2, 16384, 2048], P('dp', 'expert'), may hold values from -3 to 3
- gates: bfloat16 [2, 128, 128, 3], P('dp', 'expert'), may hold values from 0.049804688 to 1
- slot_index: int32 [2, 128, 128, 3], P('dp', 'expert'), may hold values from 0 to 127, as said below
- slot_count: int32 [2, 128, 128], P('dp', 'expert'), may hold values from 1 to 3, as said below
- up_weight: bfloat16 [128, 2048, 768], P('expert', None, 'dp'), may hold values from -0.125 to 0.125
- down_weight: bfloat16 [128, 768, 2048], P('expert', 'dp'), may hold values from -0.21875 to 0.21875
Outputs:
- d_tokens: bfloat16 [2, 16384, 2048], P('dp', 'expert')
- d_gate: bfloat16 [2, 128, 128, 3], P('dp', 'expert')
- d_up: bfloat16 [128, 2048, 768], P('expert', None, 'dp')
- d_down: bfloat16 [128, 768, 2048], P('expert', 'dp')
Inputs may be any that keep to these rules, and one draw needn't show every extreme that they name: `slot_index`: within each block the first slot_count entries are different rows; the other entries are rows too. `slot_count`: for each batch and expert the counts over all source devices sum to 256.
All inputs are finite; a program needn't handle non-finite values.
Results may differ from a plain program's by a relative error of at most 0.015.
Values may be sent and summed in bfloat16 or wider, within the bound.
A program may use at most 128 MiB of HBM per device.

v0:
```python
import jax
import jax.numpy as jnp
from jax import lax
from jax.sharding import PartitionSpec as P


def expert_backward(rows_in, rows_grad, scale, live_mask, w_up, w_down):
    hidden = jnp.dot(rows_in, w_up, preferred_element_type=jnp.float32)
    sigmoid_h = jax.nn.sigmoid(hidden)
    activation = (hidden * sigmoid_h).astype(jnp.bfloat16)
    expert_out = jnp.dot(activation, w_down, preferred_element_type=jnp.float32)
    d_gate = live_mask * jnp.sum(rows_grad.astype(jnp.float32) * expert_out, axis=1)
    upstream = lax.dot_general(
        rows_grad, w_down, (((1,), (1,)), ((), ())), preferred_element_type=jnp.float32
    )
    d_hidden = (
        scale[:, None] * upstream * (sigmoid_h * (1.0 + hidden * (1.0 - sigmoid_h)))
    ).astype(jnp.bfloat16)
    scaled = (scale[:, None] * activation.astype(jnp.float32)).astype(jnp.bfloat16)
    d_down = lax.dot_general(
        scaled, rows_grad, (((0,), (0,)), ((), ())), preferred_element_type=jnp.float32
    )
    d_up = lax.dot_general(
        rows_in, d_hidden, (((0,), (0,)), ((), ())), preferred_element_type=jnp.float32
    )
    d_rows = lax.dot_general(
        d_hidden, w_up, (((1,), (1,)), ((), ())), preferred_element_type=jnp.float32
    )
    return (d_rows, d_gate, d_up, d_down)


def run_rows(rows_in, rows_grad, gate_rows, live_rows, w_up, w_down):
    live_mask = live_rows.astype(jnp.float32)
    scale = gate_rows.astype(jnp.float32) * live_mask
    d_rows, d_gate, d_up, d_down = expert_backward(
        rows_in, rows_grad, scale, live_mask, w_up, w_down
    )
    return (d_rows, d_gate, d_up, d_down)


def per_device(tokens, grad_out, gates, slot_index, slot_count, up_weight, down_weight):
    own_tokens = tokens[0]
    own_grads = grad_out[0]
    picks = slot_index[0, 0]
    experts, slots = picks.shape
    width = own_tokens.shape[1]
    total = experts * slots
    flat = picks.reshape(-1)
    sent_in = jnp.take(own_tokens, flat, axis=0).reshape(experts, slots, width)
    sent_grad = jnp.take(own_grads, flat, axis=0).reshape(experts, slots, width)
    live = (
        lax.broadcasted_iota(jnp.int32, (experts, slots), 1) < slot_count[0, 0][:, None]
    ).astype(jnp.bfloat16)
    rows_in, rows_grad, gate_rows, live_rows = (
        lax.all_to_all(sent_in, "expert", split_axis=0, concat_axis=0, tiled=True),
        lax.all_to_all(sent_grad, "expert", split_axis=0, concat_axis=0, tiled=True),
        lax.all_to_all(gates[0, 0], "expert", split_axis=0, concat_axis=0, tiled=True),
        lax.all_to_all(live, "expert", split_axis=0, concat_axis=0, tiled=True),
    )
    full_up, full_down = (
        lax.all_gather(up_weight[0], "dp", axis=1, tiled=True),
        lax.all_gather(down_weight[0], "dp", axis=0, tiled=True),
    )
    d_rows, d_gate, d_up, d_down = run_rows(
        rows_in.reshape(total, width),
        rows_grad.reshape(total, width),
        gate_rows.reshape(total),
        live_rows.reshape(total),
        full_up,
        full_down,
    )
    d_up, d_down = (
        lax.psum_scatter(d_up, "dp", scatter_dimension=1, tiled=True),
        lax.psum_scatter(d_down, "dp", scatter_dimension=0, tiled=True),
    )
    d_rows = d_rows.reshape(experts, slots, width)
    d_gate = d_gate.reshape(experts, slots)
    back_rows, back_gate = (
        lax.all_to_all(
            d_rows.astype(jnp.bfloat16), "expert", split_axis=0, concat_axis=0, tiled=True
        ),
        lax.all_to_all(
            d_gate.astype(jnp.bfloat16), "expert", split_axis=0, concat_axis=0, tiled=True
        ),
    )
    summed = (
        jnp.zeros((own_tokens.shape[0], width), jnp.float32)
        .at[flat]
        .add(back_rows.reshape(total, width).astype(jnp.float32))
    )
    return (
        summed.astype(jnp.bfloat16)[None],
        back_gate[None, None],
        d_up.astype(jnp.bfloat16)[None],
        d_down.astype(jnp.bfloat16)[None],
    )


def solution(mesh):
    in_specs = (
        P("dp", "expert", None),
        P("dp", "expert", None),
        P("dp", "expert", None, None),
        P("dp", "expert", None, None),
        P("dp", "expert", None),
        P("expert", None, "dp"),
        P("expert", "dp", None),
    )
    out_specs = (
        P("dp", "expert", None),
        P("dp", "expert", None, None),
        P("expert", None, "dp"),
        P("expert", "dp", None),
    )
    return jax.shard_map(
        per_device, mesh=mesh, in_specs=in_specs, out_specs=out_specs, check_vma=False
    )
```

profile of v0, /device:TPU:32, one launch (start us, length us, event | category | flops | bytes accessed | tf_op | source)
XLA Modules:
  0.0 306.4 jit_solution(2039605217057924308)
XLA Ops:
  7.2 0.0 copy-start
  7.2 1.5 compare_convert_fusion
  8.7 15.0 %all-to-all-start.1 = ((bf16[128,1,3]{2,1,0:T(2,128)(2,1)}), bf16[128,1,3]{2,1,0:T(2,128)(2,1)S(1)}, u32[]{:S(2)}, u32[]{:S(2)}) async-start(bf16[128,1,3]{2,1,0:T(2,128)(2,1)} %compare_convert_fusion), calls=%async_computation.1 | async-start | bytes 131072 | tf_op jit(solution)/shard_map/all_to_all | solution.py:58
  23.7 0.8 copy.29
  24.5 0.2 reshape_squeeze.6
  24.8 0.0 copy-done
  24.8 0.0 copy-start.1
  24.8 3.1 %gather_fusion.1 = bf16[384,2048]{1,0:T(8,128)(2,1)} fusion(bf16[128,2048]{1,0:T(8,128)(2,1)S(1)} %bitcast.43, s32[1024]{0:T(1024)S(1)} %pad_clamp_fusion), kind=kCustom, calls=%fused_computation.1.clone | custom fusion | bytes 3147264 | tf_op jit(solution)/shard_map/jit(_take)/gather | solution.py:49
  27.9 0.0 copy-done.1
  27.9 0.0 copy-start.3
  27.9 3.1 %gather_fusion = bf16[384,2048]{1,0:T(8,128)(2,1)} fusion(bf16[128,2048]{1,0:T(8,128)(2,1)S(1)} %bitcast.44, s32[1024]{0:T(1024)S(1)} %pad_clamp_fusion), kind=kCustom, calls=%fused_computation.clone | custom fusion | bytes 3147264 | tf_op jit(solution)/shard_map/jit(_take)/gather | solution.py:50
  31.0 0.0 copy-done.3
  31.0 0.8 copy.30
  31.8 3.3 %all-to-all-done.1 = bf16[128,1,3]{2,1,0:T(2,128)(2,1)S(1)} async-done(((bf16[128,1,3]{2,1,0:T(2,128)(2,1)}), bf16[128,1,3]{2,1,0:T(2,128)(2,1)S(1)}, u32[]{:S(2)}, u32[]{:S(2)}) %all-to-all-start.1) | async-done | bytes 800 | tf_op jit(solution)/shard_map/all_to_all | solution.py:58
  35.1 10.4 %all-to-all-start = ((bf16[128,1,3]{2,1,0:T(2,128)(2,1)}), bf16[128,1,3]{2,1,0:T(2,128)(2,1)S(1)}, u32[]{:S(2)}, u32[]{:S(2)}) async-start(bf16[128,1,3]{2,1,0:T(2,128)(2,1)} %copy.30), calls=%async_computation | async-start | bytes 131072 | tf_op jit(solution)/shard_map/all_to_all | solution.py:57
  45.5 3.4 %broadcast_select_fusion = (bf16[384,2048]{1,0:T(8,128)(2,1)}, bf16[384,2048]{1,0:T(8,128)(2,1)S(1)}) fusion(bf16[384,2048]{1,0:T(8,128)(2,1)} %gather_fusion.1, pred[384]{0:T(512)(128)(4,1)S(1)} %compare_and_fusion, bf16[384,2048]{1,0:T(8,128)(2,1)} %gather_fusion), kind=kLoop, calls=%fused_computation.15 | loop fusion | flops 1572864 | bytes 6291840 | tf_op jit(solution)/shard_map/jit(_take)/select_n | solution.py:49
  48.9 2.3 reshape.126
  51.2 5.7 %all-to-all-done = bf16[128,1,3]{2,1,0:T(2,128)(2,1)S(1)} async-done(((bf16[128,1,3]{2,1,0:T(2,128)(2,1)}), bf16[128,1,3]{2,1,0:T(2,128)(2,1)S(1)}, u32[]{:S(2)}, u32[]{:S(2)}) %all-to-all-start) | async-done | bytes 800 | tf_op jit(solution)/shard_map/all_to_all | solution.py:57
  57.0 8.0 %all-to-all-start.2 = ((bf16[128,3,2048]{2,1,0:T(4,128)(2,1)}), bf16[128,3,2048]{2,1,0:T(4,128)(2,1)S(1)}, u32[]{:S(2)}, u32[]{:S(2)}) async-start(bf16[128,3,2048]{2,1,0:T(4,128)(2,1)} %reshape.126), calls=%async_computation.2 | async-start | bytes 4194304 | tf_op jit(solution)/shard_map/all_to_all | solution.py:56
  65.0 0.0 all-gather.7.cloned.1.call-start
  65.0 0.7 all-gather.7.cloned.1.call-update
  65.7 5.2 %reshape.128 = bf16[128,3,2048]{2,1,0:T(4,128)(2,1)} reshape(bf16[384,2048]{1,0:T(8,128)(2,1)} %get-tuple-element.15) | data formatting | bytes 3145728 | tf_op jit(solution)/shard_map/reshape | solution.py:49
  70.9 46.4 %all-to-all-done.2 = bf16[128,3,2048]{2,1,0:T(4,128)(2,1)S(1)} async-done(((bf16[128,3,2048]{2,1,0:T(4,128)(2,1)}), bf16[128,3,2048]{2,1,0:T(4,128)(2,1)S(1)}, u32[]{:S(2)}, u32[]{:S(2)}) %all-to-all-start.2) | async-done | bytes 1572896 | tf_op jit(solution)/shard_map/all_to_all | solution.py:56
  117.3 6.9 %all-to-all-start.3 = ((bf16[128,3,2048]{2,1,0:T(4,128)(2,1)}), bf16[128,3,2048]{2,1,0:T(4,128)(2,1)}, u32[]{:S(2)}, u32[]{:S(2)}) async-start(bf16[128,3,2048]{2,1,0:T(4,128)(2,1)} %reshape.128), calls=%async_computation.3 | async-start | bytes 4194304 | tf_op jit(solution)/shard_map/all_to_all | solution.py:55
  124.2 0.0 all-gather.5.cloned.1.call-start
  124.2 0.7 all-gather.5.cloned.1.call-update
  124.9 0.2 reduce-scatter.3.cloned.1.call-start
  125.2 0.1 copy.32
  125.2 0.1 copy.31
  125.3 2.5 reshape.127
  127.9 48.0 %all-to-all-done.3 = bf16[128,3,2048]{2,1,0:T(4,128)(2,1)} async-done(((bf16[128,3,2048]{2,1,0:T(4,128)(2,1)}), bf16[128,3,2048]{2,1,0:T(4,128)(2,1)}, u32[]{:S(2)}, u32[]{:S(2)}) %all-to-all-start.3) | async-done | bytes 1572896 | tf_op jit(solution)/shard_map/all_to_all | solution.py:55
  175.9 3.9 %reshape.129 = bf16[384,2048]{1,0:T(8,128)(2,1)S(1)} reshape(bf16[128,3,2048]{2,1,0:T(4,128)(2,1)} %all-to-all-done.3) | data formatting | bytes 3145728 | tf_op jit(solution)/shard_map/reshape | solution.py:65
  179.8 0.0 all-gather.7.cloned.1.call-done
  179.8 4.3 %fusion.2 = f32[384,768]{1,0:T(8,128)} fusion(bf16[384,2048]{1,0:T(8,128)(2,1)S(1)} %reshape.129, bf16[1,2048,768]{2,1,0:T(8,128)(2,1)} %all-gather.7.cloned.1.call-done), kind=kOutput, calls=%fused_computation.5 | convolution fusion | flops 1207959552 | bytes 5898240 | tf_op jit(solution)/shard_map/dot_general | solution.py:8
  184.1 0.0 all-gather.5.cloned.1.call-done
  184.1 4.2 %multiply_reduce_fusion = f32[384]{0:T(512)S(1)} fusion(bf16[384,2048]{1,0:T(8,128)(2,1)} %reshape.127, bf16[1,768,2048]{2,1,0:T(8,128)(2,1)} %all-gather.5.cloned.1.call-done, f32[384,768]{1,0:T(8,128)} %fusion.2), kind=kOutput, calls=%fused_computation.11 | convolution fusion | flops 1211793024 | bytes 5899776 | tf_op jit(solution)/shard_map/dot_general | solution.py:11
  188.3 0.2 reduce_sum.12
  188.5 0.1 copy.35
  188.6 0.1 copy.33
  188.7 0.2 mul.45
  189.0 4.3 %fusion.19 = bf16[384,768]{1,0:T(8,128)(2,1)S(1)} fusion(bf16[384,2048]{1,0:T(8,128)(2,1)} %reshape.127, bf16[1,768,2048]{2,1,0:T(8,128)(2,1)} %all-gather.5.cloned.1.call-done, f32[384,768]{1,0:T(8,128)} %fusion.2, f32[384]{0:T(512)S(1)} %mul.45), kind=kOutput, calls=%fused_computation.19 | convolution fusion | flops 1210908672 | bytes 6489600 | tf_op jit(solution)/shard_map/dot_general | solution.py:13
  193.2 4.5 %fusion.27 = f32[2048,768]{1,0:T(8,128)} fusion(bf16[384,2048]{1,0:T(8,128)(2,1)S(1)} %reshape.129, bf16[384,768]{1,0:T(8,128)(2,1)S(1)} %fusion.19), kind=kOutput, calls=%fused_computation.36 | convolution fusion | flops 1207959552 | bytes 8454144 | tf_op jit(solution)/shard_map/dot_general | solution.py:23
  197.7 0.0 copy-start.2
  197.7 0.0 reduce-scatter.3.cloned.1.call-update
  197.8 0.0 reduce-scatter.5.cloned.1.call-start
  197.8 1.3 copy-done.2
  199.1 6.7 %fusion.22 = f32[768,2048]{1,0:T(8,128)} fusion(bf16[384,2048]{1,0:T(8,128)(2,1)S(1)} %copy-done.2, f32[384]{0:T(512)S(1)} %mul.45, f32[384,768]{1,0:T(8,128)} %fusion.2), kind=kOutput, calls=%fused_computation.23 | convolution fusion | flops 1210318848 | bytes 9045504 | tf_op jit(solution)/shard_map/dot_general | solution.py:20
  205.9 0.0 reduce-scatter.5.cloned.1.call-update
  205.9 0.8 copy.36
  206.7 5.5 %all-to-all-start.5 = ((bf16[128,1,3]{2,1,0:T(2,128)(2,1)}), bf16[128,1,3]{2,1,0:T(2,128)(2,1)S(1)}, u32[]{:S(2)}, u32[]{:S(2)}) async-start(bf16[128,1,3]{2,1,0:T(2,128)(2,1)} %copy.36), calls=%async_computation.5 | async-start | bytes 131072 | tf_op jit(solution)/shard_map/all_to_all | solution.py:82
  212.2 3.3 %fusion.10 = bf16[384,2048]{1,0:T(8,128)(2,1)S(1)} fusion(bf16[384,768]{1,0:T(8,128)(2,1)S(1)} %fusion.19, bf16[1,2048,768]{2,1,0:T(8,128)(2,1)} %all-gather.7.cloned.1.call-done), kind=kOutput, calls=%fused_computation.12 | convolution fusion | flops 1208745984 | bytes 5308416 | tf_op jit(solution)/shard_map/dot_general | solution.py:26
  215.5 2.3 convert_element_type.73
  217.8 5.7 %all-to-all-done.5 = bf16[128,1,3]{2,1,0:T(2,128)(2,1)S(1)} async-done(((bf16[128,1,3]{2,1,0:T(2,128)(2,1)}), bf16[128,1,3]{2,1,0:T(2,128)(2,1)S(1)}, u32[]{:S(2)}, u32[]{:S(2)}) %all-to-all-start.5) | async-done | bytes 800 | tf_op jit(solution)/shard_map/all_to_all | solution.py:82
  223.5 8.3 %all-to-all-start.4 = ((bf16[128,3,2048]{2,1,0:T(4,128)(2,1)}), bf16[128,3,2048]{2,1,0:T(4,128)(2,1)S(1)}, u32[]{:S(2)}, u32[]{:S(2)}) async-start(bf16[128,3,2048]{2,1,0:T(4,128)(2,1)} %convert_element_type.73), calls=%async_computation.4 | async-start | bytes 4194304 | tf_op jit(solution)/shard_map/all_to_all | solution.py:79
  231.8 0.2 reshape_squeeze.5
  232.1 0.7 copy.37
  232.7 50.3 %all-to-all-done.4 = bf16[128,3,2048]{2,1,0:T(4,128)(2,1)S(1)} async-done(((bf16[128,3,2048]{2,1,0:T(4,128)(2,1)}), bf16[128,3,2048]{2,1,0:T(4,128)(2,1)S(1)}, u32[]{:S(2)}, u32[]{:S(2)}) %all-to-all-start.4) | async-done | bytes 1572896 | tf_op jit(solution)/shard_map/all_to_all | solution.py:79
  283.0 2.7 reshape.151
  285.7 6.8 %scatter_custom_fusion = f32[128,2048]{1,0:T(8,128)S(1)} fusion(s32[384]{0:T(512)S(1)} %fusion.26, f32[384,2048]{1,0:T(8,128)} %reshape.151, f32[]{:T(128)} %constant.0.clone.1), kind=kCustom, calls=%fused_computation.26 | custom fusion | flops 786432 | bytes 1049088 | tf_op jit(solution)/shard_map/scatter-add | solution.py:89
  292.6 0.9 convert_bitcast_fusion.2
  293.4 0.0 reduce-scatter.3.cloned.1.call-done
  293.4 3.2 %convert_bitcast_fusion.1 = bf16[1,2048,384]{2,1,0:T(8,128)(2,1)} fusion(f32[2048,384]{1,0:T(8,128)} %reduce-scatter.3.cloned.1.call-done), kind=kLoop, calls=%fused_computation.14 | loop fusion | flops 786432 | bytes 4718592 | tf_op jit(solution)/shard_map/broadcast_in_dim | solution.py:94
  296.6 0.0 reduce-scatter.5.cloned.1.call-done
  296.6 3.3 %convert_bitcast_fusion = bf16[1,384,2048]{2,1,0:T(8,128)(2,1)} fusion(f32[384,2048]{1,0:T(8,128)} %reduce-scatter.5.cloned.1.call-done), kind=kLoop, calls=%fused_computation.13 | loop fusion | flops 786432 | bytes 4718592 | tf_op jit(solution)/shard_map/broadcast_in_dim | solution.py:95
  (5 shorter events, 0.1 us)
Async XLA Ops:
  7.2 17.6 %copy-start = (bf16[1,128,2048]{2,1,0:T(8,128)(2,1)S(1)}, bf16[1,128,2048]{2,1,0:T(8,128)(2,1)}, u32[]{:S(2)}) copy-start(bf16[1,128,2048]{2,1,0:T(8,128)(2,1)} %param.9) | copy-start | bytes 1572868
  8.7 26.4 %all-to-all-start.1 = ((bf16[128,1,3]{2,1,0:T(2,128)(2,1)}), bf16[128,1,3]{2,1,0:T(2,128)(2,1)S(1)}, u32[]{:S(2)}, u32[]{:S(2)}) async-start(bf16[128,1,3]{2,1,0:T(2,128)(2,1)} %compare_convert_fusion), calls=%async_computation.1 | async-start | bytes 131072 | tf_op jit(solution)/shard_map/all_to_all | solution.py:58
  24.8 3.1 %copy-start.1 = (bf16[1,128,2048]{2,1,0:T(8,128)(2,1)S(1)}, bf16[1,128,2048]{2,1,0:T(8,128)(2,1)}, u32[]{:S(2)}) copy-start(bf16[1,128,2048]{2,1,0:T(8,128)(2,1)} %param.10) | copy-start | bytes 1572868
  27.9 3.1 %copy-start.3 = (bf16[1,1,128,3]{2,3,1,0:T(4,128)(2,1)S(1)}, bf16[1,1,128,3]{2,3,1,0:T(4,128)(2,1)}, u32[]{:S(2)}) copy-start(bf16[1,1,128,3]{2,3,1,0:T(4,128)(2,1)} %param.11) | copy-start | bytes 2308
  35.1 21.9 %all-to-all-start = ((bf16[128,1,3]{2,1,0:T(2,128)(2,1)}), bf16[128,1,3]{2,1,0:T(2,128)(2,1)S(1)}, u32[]{:S(2)}, u32[]{:S(2)}) async-start(bf16[128,1,3]{2,1,0:T(2,128)(2,1)} %copy.30), calls=%async_computation | async-start | bytes 131072 | tf_op jit(solution)/shard_map/all_to_all | solution.py:57
  57.0 60.3 %all-to-all-start.2 = ((bf16[128,3,2048]{2,1,0:T(4,128)(2,1)}), bf16[128,3,2048]{2,1,0:T(4,128)(2,1)S(1)}, u32[]{:S(2)}, u32[]{:S(2)}) async-start(bf16[128,3,2048]{2,1,0:T(4,128)(2,1)} %reshape.126), calls=%async_computation.2 | async-start | bytes 4194304 | tf_op jit(solution)/shard_map/all_to_all | solution.py:56
  65.0 114.9 %all-gather.7.cloned.1.call-start = ((), (), s32[]{:S(2)}) async-start(), calls=%async_computation.11 | async-start | bytes 4718592 | tf_op jit(solution)/shard_map/all_gather | solution.py:61
  117.3 58.6 %all-to-all-start.3 = ((bf16[128,3,2048]{2,1,0:T(4,128)(2,1)}), bf16[128,3,2048]{2,1,0:T(4,128)(2,1)}, u32[]{:S(2)}, u32[]{:S(2)}) async-start(bf16[128,3,2048]{2,1,0:T(4,128)(2,1)} %reshape.128), calls=%async_computation.3 | async-start | bytes 4194304 | tf_op jit(solution)/shard_map/all_to_all | solution.py:55
  124.2 59.9 %all-gather.5.cloned.1.call-start = ((), (), s32[]{:S(2)}) async-start(), calls=%async_computation.10 | async-start | bytes 4718592 | tf_op jit(solution)/shard_map/all_gather | solution.py:62
  124.9 168.5 %reduce-scatter.3.cloned.1.call-start = ((), (), s32[]{:S(2)}) async-start(), calls=%async_computation.8 | async-start | bytes 9437184 | tf_op jit(solution)/shard_map/reduce_scatter | solution.py:73
  197.7 1.4 copy-start.2
  197.8 98.9 %reduce-scatter.5.cloned.1.call-start = ((), (), s32[]{:S(2)}) async-start(), calls=%async_computation.9 | async-start | bytes 9437184 | tf_op jit(solution)/shard_map/reduce_scatter | solution.py:74
  206.7 16.9 %all-to-all-start.5 = ((bf16[128,1,3]{2,1,0:T(2,128)(2,1)}), bf16[128,1,3]{2,1,0:T(2,128)(2,1)S(1)}, u32[]{:S(2)}, u32[]{:S(2)}) async-start(bf16[128,1,3]{2,1,0:T(2,128)(2,1)} %copy.36), calls=%async_computation.5 | async-start | bytes 131072 | tf_op jit(solution)/shard_map/all_to_all | solution.py:82
  223.5 59.4 %all-to-all-start.4 = ((bf16[128,3,2048]{2,1,0:T(4,128)(2,1)}), bf16[128,3,2048]{2,1,0:T(4,128)(2,1)S(1)}, u32[]{:S(2)}, u32[]{:S(2)}) async-start(bf16[128,3,2048]{2,1,0:T(4,128)(2,1)} %convert_element_type.73), calls=%async_computation.4 | async-start | bytes 4194304 | tf_op jit(solution)/shard_map/all_to_all | solution.py:79
Sparse Core Ops, SparseCore 0:
  67.6 18.6 all-gather.6
  126.8 18.7 all-gather.4
  197.9 13.7 reduce-scatter.2
  214.3 21.0 reduce-scatter.4
where the time goes:
time: 307 us; the launch traced here: 306 us
  waiting for transfers between devices  161 us (52%)
  starting transfers between devices  54.5 us (18%)
  local copies, waits for them, and re-layouts  30.7 us (10%)
  matrix products  27.3 us (9%)
  other arithmetic  19.2 us (6%)
  between operations  13.9 us (5%)
    all_to_all x1, waiting for transfers between devices, per_device(): lax.all_to_all(d_rows.astype(jnp.bfloat16), 'expert', split_axis=0, conca...  50.3 us
    all_to_all x1, waiting for transfers between devices, per_device(): lax.all_to_all(sent_in, 'expert', split_axis=0, concat_axis=0, tiled=True)  48 us
    all_to_all x1, waiting for transfers between devices, per_device(): lax.all_to_all(sent_grad, 'expert', split_axis=0, concat_axis=0, tiled=True)  46.4 us
    all_to_all x1, starting transfers between devices, per_device(): lax.all_to_all(live, 'expert', split_axis=0, concat_axis=0, tiled=True)  15 us
    all_to_all x1, starting transfers between devices, per_device(): lax.all_to_all(gates[0, 0], 'expert', split_axis=0, concat_axis=0, tiled=...  10.4 us
    all_to_all x1, starting transfers between devices, per_device(): lax.all_to_all(d_rows.astype(jnp.bfloat16), 'expert', split_axis=0, conca...  8.27 us
    all_to_all x1, starting transfers between devices, per_device(): lax.all_to_all(sent_grad, 'expert', split_axis=0, concat_axis=0, tiled=True)  8 us
    all_to_all x1, starting transfers between devices, per_device(): lax.all_to_all(sent_in, 'expert', split_axis=0, concat_axis=0, tiled=True)  6.88 us
  transfers between devices with their start and end apart: 10, of which 6 were waited for; matrix products, arithmetic and copies ran while one was open for 19% of the time, Pallas kernels for 0%

commit v1 on v0

v1 whole, which is shorter than its diff:
```python
import jax
import jax.numpy as jnp
from jax import lax
from jax.experimental import pallas as pl
from jax.experimental.pallas import tpu as pltpu
from jax.sharding import PartitionSpec as P

MESH = pl.DeviceIdType.MESH
NX, NY, NZ = 4, 4, 8
N = NX * NY * NZ
LANES = 128
SUB = 16


def partner(me, step, sign):
    dz, dy, dx = step % NZ, (step // NZ) % NY, step // (NZ * NY)
    x, y, z = me % NX, (me // NX) % NY, me // (NX * NY)
    z = (z + sign * dz + NZ) % NZ
    y = (y + sign * dy + NY) % NY
    x = (x + sign * dx + NX) % NX
    return (z * NY + y) * NX + x


def enter(me):
    barrier = pltpu.get_barrier_semaphore()

    def greet(step, carry):
        pl.semaphore_signal(
            barrier,
            inc=1,
            device_id={"expert": lax.rem(me + step, N)},
            device_id_type=MESH,
        )
        return carry

    lax.fori_loop(1, N, greet, 0)
    pl.semaphore_wait(barrier, N - 1)


def forward_kernel(idx_ref, scale_ref, tok_ref, grad_ref, out_ref, send_ref, send_sem, recv_sem, own_sem):
    me = lax.axis_index("expert")
    enter(me)
    slots = send_ref.shape[1] // 2

    def fill(target):
        for k in range(slots):
            row = idx_ref[target * slots + k]
            send_ref[target, k] = tok_ref[row]
            scaled = grad_ref[row].astype(jnp.float32) * scale_ref[target * slots + k]
            send_ref[target, slots + k] = scaled.astype(jnp.bfloat16)

    fill(me)
    own = pltpu.make_async_copy(send_ref.at[me], out_ref.at[me], own_sem)
    own.start()

    def step(i, carry):
        target = partner(me, i, 1)
        fill(target)
        pltpu.make_async_remote_copy(
            src_ref=send_ref.at[target],
            dst_ref=out_ref.at[me],
            send_sem=send_sem,
            recv_sem=recv_sem,
            device_id={"expert": target},
            device_id_type=MESH,
        ).start()
        return carry

    lax.fori_loop(1, N, step, 0)
    rest = send_ref.at[pl.ds(0, N - 1)]
    pltpu.make_async_copy(rest, rest, recv_sem).wait()
    pltpu.make_async_copy(rest, rest, send_sem).wait()
    own.wait()


def return_kernel(rows_ref, gate_ref, out_ref, gout_ref, send_sem, recv_sem, gsend_sem, grecv_sem, own_sem):
    me = lax.axis_index("expert")
    enter(me)
    own = pltpu.make_async_copy(rows_ref.at[me], out_ref.at[me], own_sem.at[0])
    own.start()
    gown = pltpu.make_async_copy(gate_ref.at[me], gout_ref.at[me], own_sem.at[1])
    gown.start()

    def step(i, carry):
        target = partner(me, i, 1)
        pltpu.make_async_remote_copy(
            src_ref=rows_ref.at[target],
            dst_ref=out_ref.at[me],
            send_sem=send_sem,
            recv_sem=recv_sem,
            device_id={"expert": target},
            device_id_type=MESH,
        ).start()
        pltpu.make_async_remote_copy(
            src_ref=gate_ref.at[target],
            dst_ref=gout_ref.at[me],
            send_sem=gsend_sem,
            recv_sem=grecv_sem,
            device_id={"expert": target},
            device_id_type=MESH,
        ).start()
        return carry

    lax.fori_loop(1, N, step, 0)
    for ref, sems in ((rows_ref, (recv_sem, send_sem)), (gate_ref, (grecv_sem, gsend_sem))):
        rest = ref.at[pl.ds(0, N - 1)]
        for sem in sems:
            pltpu.make_async_copy(rest, rest, sem).wait()
    own.wait()
    gown.wait()


def per_device(tokens, grad_out, gates, slot_index, slot_count, up_weight, down_weight):
    experts, slots = slot_index.shape[2:]
    width = tokens.shape[2]
    total = experts * slots
    held = tokens.shape[1]
    flat = slot_index[0, 0].reshape(-1)
    live = lax.broadcasted_iota(jnp.int32, (experts, slots), 1) < slot_count[0, 0][:, None]
    live = live.astype(jnp.float32).reshape(total)
    scale = gates[0, 0].astype(jnp.float32).reshape(total) * live

    vmem = pl.BlockSpec(memory_space=pltpu.VMEM)
    smem = pl.BlockSpec(memory_space=pltpu.SMEM)
    block = (experts, 2 * slots, SUB, LANES)
    received = pl.pallas_call(
        forward_kernel,
        out_shape=jax.ShapeDtypeStruct(block, jnp.bfloat16),
        in_specs=[smem, smem, vmem, vmem],
        out_specs=vmem,
        scratch_shapes=[
            pltpu.VMEM(block, jnp.bfloat16),
            pltpu.SemaphoreType.DMA,
            pltpu.SemaphoreType.DMA,
            pltpu.SemaphoreType.DMA,
        ],
        compiler_params=pltpu.CompilerParams(
            collective_id=0, has_side_effects=True, vmem_limit_bytes=40 << 20
        ),
    )(
        flat,
        scale,
        tokens[0].reshape(held, SUB, LANES),
        grad_out[0].reshape(held, SUB, LANES),
    )
    rows_in = received[:, :slots].reshape(total, width)
    rows_grad = received[:, slots:].reshape(total, width)

    w_up = lax.all_gather(up_weight[0], "dp", axis=1, tiled=True)
    w_down = lax.all_gather(down_weight[0], "dp", axis=0, tiled=True)
    hidden = jnp.dot(rows_in, w_up, preferred_element_type=jnp.float32)
    gate_h = jax.nn.sigmoid(hidden)
    activation = (hidden * gate_h).astype(jnp.bfloat16)
    upstream = lax.dot_general(
        rows_grad, w_down, (((1,), (1,)), ((), ())), preferred_element_type=jnp.float32
    )
    d_hidden = (upstream * (gate_h * (1.0 + hidden * (1.0 - gate_h)))).astype(jnp.bfloat16)
    d_gate = jnp.sum(activation.astype(jnp.float32) * upstream, axis=1)
    d_rows = lax.dot_general(
        d_hidden, w_up, (((1,), (1,)), ((), ())), preferred_element_type=jnp.float32
    ).astype(jnp.bfloat16)
    d_down = lax.dot_general(
        activation, rows_grad, (((0,), (0,)), ((), ())), preferred_element_type=jnp.float32
    )
    d_up = lax.dot_general(
        rows_in, d_hidden, (((0,), (0,)), ((), ())), preferred_element_type=jnp.float32
    )
    d_up = lax.psum_scatter(d_up, "dp", scatter_dimension=1, tiled=True)
    d_down = lax.psum_scatter(d_down, "dp", scatter_dimension=0, tiled=True)

    gate_block = jnp.pad(d_gate.reshape(experts, 1, slots), ((0, 0), (0, 0), (0, LANES - slots)))
    back, gate_back = pl.pallas_call(
        return_kernel,
        out_shape=(
            jax.ShapeDtypeStruct((experts, slots, SUB, LANES), jnp.bfloat16),
            jax.ShapeDtypeStruct((experts, 1, LANES), jnp.float32),
        ),
        in_specs=[vmem, vmem],
        out_specs=(vmem, vmem),
        scratch_shapes=[pltpu.SemaphoreType.DMA] * 4 + [pltpu.SemaphoreType.DMA((2,))],
        compiler_params=pltpu.CompilerParams(
            collective_id=1, has_side_effects=True, vmem_limit_bytes=40 << 20
        ),
    )(d_rows.reshape(experts, slots, SUB, LANES), gate_block)

    spread = (flat[None, :] == jnp.arange(held, dtype=jnp.int32)[:, None]).astype(jnp.bfloat16)
    summed = jnp.dot(spread, back.reshape(total, width), preferred_element_type=jnp.float32)
    inverse = jnp.where(live > 0, 1.0 / jnp.where(live > 0, scale, 1.0), 0.0)
    d_gates = gate_back[:, 0, :slots] * inverse.reshape(experts, slots)
    return (
        summed.astype(jnp.bfloat16)[None],
        d_gates.astype(jnp.bfloat16)[None, None],
        d_up.astype(jnp.bfloat16)[None],
        d_down.astype(jnp.bfloat16)[None],
    )


def solution(mesh):
    in_specs = (
        P("dp", "expert", None),
        P("dp", "expert", None),
        P("dp", "expert", None, None),
        P("dp", "expert", None, None),
        P("dp", "expert", None),
        P("expert", None, "dp"),
        P("expert", "dp", None),
    )
    out_specs = (
        P("dp", "expert", None),
        P("dp", "expert", None, None),
        P("expert", None, "dp"),
        P("expert", "dp", None),
    )
    return jax.shard_map(
        per_device, mesh=mesh, in_specs=in_specs, out_specs=out_specs, check_vma=False
    )
```

time: 307 us -> 177 us (0.58)
  waiting for transfers between devices: 161 us -> 1.45 us
  Pallas kernels: 0 us -> 127 us
  starting transfers between devices: 54.5 us -> 0.16 us
  local copies, waits for them, and re-layouts: 30.7 us -> 5.83 us
  other arithmetic: 19.2 us -> 6.65 us
  matrix products: 27.3 us -> 21.7 us
    all_to_all x6 -> x0, waiting for transfers between devices: 159 us -> none  [the longest x1 50.3 us: per_device(): lax.all_to_all(d_rows.astype(jnp.bfloat16), 'expert', split_axis=0, conca...]
    pallas_call x0 -> x2, Pallas kernels: none -> 127 us  [the longest x1 81.9 us: per_device(): pl.pallas_call(forward_kernel, out_shape=jax.ShapeDtypeStruct(block, jnp....]
    all_to_all x6 -> x0, starting transfers between devices: 54.1 us -> none  [the longest x1 15 us: per_device(): lax.all_to_all(live, 'expert', split_axis=0, concat_axis=0, tiled=True)]
    reshape x4 -> x1, local copies, waits for them, and re-layouts: 13.9 us -> 0.2 us  [per_device(): d_gate.reshape(experts, 1, slots)]
    scatter-add x1 -> x0, other arithmetic: 6.85 us -> none  [per_device(): summed = jnp.zeros((own_tokens.shape[0], width), jnp.float32).at[flat].ad...]
    gather x2 -> x0, local copies, waits for them, and re-layouts: 6.21 us -> none  [the longest x1 3.11 us: per_device(): sent_in = jnp.take(own_tokens, flat, axis=0).reshape(experts, slots, width)]
    convert_element_type x3 -> x1, local copies, waits for them, and re-layouts: 5.87 us -> 0.21 us  [per_device(): scale = gates[0, 0].astype(jnp.float32).reshape(total) * live]
    dot_general x6, matrix products: 27.3 us -> 21.7 us  [the longest x1 4.56 us: per_device(): lax.dot_general(activation, rows_grad, (((0,), (0,)), ((), ())), preferre...]
  transfers between devices with their start and end apart: 10 -> 4, of which waited for: 6 -> 0; matrix products, arithmetic and copies ran while one was open for 19% -> 16% of each run, Pallas kernels for 0% -> 72%
where the time goes in v1:
time: 177 us
  Pallas kernels  127 us (72%)
  matrix products  21.7 us (12%)
  between operations  14 us (8%)
  other arithmetic  6.65 us (4%)
  local copies, waits for them, and re-layouts  5.83 us (3%)
    pallas_call x1, Pallas kernels, per_device(): pl.pallas_call(forward_kernel, out_shape=jax.ShapeDtypeStruct(block, jnp....  81.9 us
    pallas_call x1, Pallas kernels, per_device(): pl.pallas_call(return_kernel, out_shape=(jax.ShapeDtypeStruct((experts, s...  44.9 us
    dot_general x1, matrix products, per_device(): lax.dot_general(activation, rows_grad, (((0,), (0,)), ((), ())), preferre...  4.56 us
    dot_general x1, matrix products, per_device(): lax.dot_general(rows_in, d_hidden, (((0,), (0,)), ((), ())), preferred_el...  4.51 us
    unnamed x22, local copies, waits for them, and re-layouts  4.41 us
    dot_general x1, matrix products, per_device(): lax.dot_general(d_hidden, w_up, (((1,), (1,)), ((), ())), preferred_eleme...  4.12 us
    dot_general x1, matrix products, per_device(): lax.dot_general(rows_grad, w_down, (((1,), (1,)), ((), ())), preferred_el...  3.98 us
  transfers between devices with their start and end apart: 4, of which 0 were waited for; matrix products, arithmetic and copies ran while one was open for 16% of the time, Pallas kernels for 72%

profile of v1, /device:TPU:32, one launch (start us, length us, event | category | flops | bytes accessed | tf_op | source)
XLA Modules:
  0.0 176.7 jit_solution(12373131517968647777)
XLA Ops:
  7.2 0.0 copy-start.4
  7.2 0.0 copy-start.6
  7.2 0.0 copy-start.5
  7.2 0.0 copy-start.2
  7.2 0.0 all-gather.7.cloned.1.call-start
  7.3 0.7 all-gather.7.cloned.1.call-update
  7.9 0.0 copy-start.3
  8.0 0.0 all-gather.5.cloned.1.call-start
  8.0 0.7 all-gather.5.cloned.1.call-update
  8.7 0.0 reduce-scatter.5.cloned.1.call-start
  8.7 0.0 copy-done.4
  8.8 0.1 iota_compare_fusion.3
  8.8 0.2 lt.32
  9.1 0.0 copy-done.6
  9.1 0.1 copy.14
  9.2 0.2 reshape.99
  9.4 0.0 copy-done.5
  9.4 0.1 copy.13
  9.5 0.2 eq.15.idx_ref
  9.8 0.0 copy-done.2
  9.8 0.1 copy.17
  9.9 0.0 copy-done.3
  9.9 0.1 copy.18
  10.0 81.9 %shard_map.102 = bf16[128,6,16,128]{3,2,1,0:T(8,128)(2,1)S(1)} custom-call(s32[384]{0:T(512)S(1)} %eq.15.idx_ref, f32[384]{0:T(512)S(1)} %broadcast_select_fusion.scale_ref, bf16[128,16,128]{2,1,0:T(8,128)(2,1)S(1)} %bitcast.62, bf16[128,16,128]{2,1,0:T(8,128)(2,1)S(1)} %bitcast.63), custom_call_target="tpu_custom_call" | custom-call | tf_op jit(solution)/shard_map/pallas_call | solution.py:126
  92.0 0.5 fusion.26
  92.5 0.0 all-gather.7.cloned.1.call-done
  92.6 3.3 %fusion.2 = f32[384,768]{1,0:T(8,128)S(1)} fusion(bf16[1,2048,768]{2,1,0:T(8,128)(2,1)} %all-gather.7.cloned.1.call-done, bf16[48,8,16,128]{3,2,1,0:T(8,128)(2,1)S(1)} %bitcast.66), kind=kOutput, calls=%fused_computation.2 | convolution fusion | flops 1207959552 | bytes 5898240 | tf_op jit(solution)/shard_map/dot_general | solution.py:151
  95.8 0.0 copy-start.7
  95.9 1.0 copy-done.7
  96.9 4.6 %fusion.15 = f32[768,2048]{1,0:T(8,128)} fusion(bf16[48,8,16,128]{3,2,1,0:T(8,128)(2,1)S(1)} %bitcast.68, f32[384,768]{1,0:T(8,128)S(1)} %fusion.2), kind=kOutput, calls=%fused_computation.14 | convolution fusion | flops 1209434112 | bytes 9043968 | tf_op jit(solution)/shard_map/dot_general | solution.py:162
  101.4 0.0 reduce-scatter.5.cloned.1.call-update
  101.4 0.0 reduce-scatter.3.cloned.1.call-start
  101.5 0.0 all-gather.5.cloned.1.call-done
  101.5 4.0 %multiply_reduce_fusion = (f32[384]{0:T(512)S(1)}, bf16[384,768]{1,0:T(8,128)(2,1)S(1)}) fusion(f32[384,768]{1,0:T(8,128)} %copy-done.7, bf16[1,768,2048]{2,1,0:T(8,128)(2,1)} %all-gather.5.cloned.1.call-done, bf16[48,8,16,128]{3,2,1,0:T(8,128)(2,1)S(1)} %bitcast.69), kind=kOutput, calls=%fused_computation.24 | convolution fusion | flops 1212087936 | bytes 6489600 | tf_op jit(solution)/shard_map/dot_general | solution.py:154
  105.5 0.0 copy-start
  105.5 0.8 copy-done
  106.3 4.5 %fusion.12 = f32[2048,768]{1,0:T(8,128)} fusion(bf16[384,768]{1,0:T(8,128)(2,1)S(1)} %get-tuple-element.19, bf16[48,8,16,128]{3,2,1,0:T(8,128)(2,1)S(1)} %bitcast.67), kind=kOutput, calls=%fused_computation.11 | convolution fusion | flops 1207959552 | bytes 8454144 | tf_op jit(solution)/shard_map/dot_general | solution.py:165
  110.8 0.0 copy-start.1
  110.8 0.0 reduce-scatter.3.cloned.1.call-update
  110.9 1.0 copy-done.1
  111.9 4.1 %fusion.18 = bf16[48,8,16,128]{3,1,2,0:T(8,128)(2,1)S(1)} fusion(bf16[384,768]{1,0:T(8,128)(2,1)S(1)} %copy-done.1, bf16[1,2048,768]{2,1,0:T(8,128)(2,1)} %all-gather.7.cloned.1.call-done), kind=kOutput, calls=%fused_computation.19 | convolution fusion | flops 1208745984 | bytes 5308416 | tf_op jit(solution)/shard_map/dot_general | solution.py:159
  116.0 0.4 copy.21
  116.4 0.2 reshape.97
  116.7 44.9 %shard_map.103 = (bf16[128,3,16,128]{3,2,1,0:T(8,128)(2,1)S(1)}, f32[128,1,128]{2,1,0:T(1,128)S(1)}) custom-call(bf16[128,3,16,128]{3,2,1,0:T(8,128)(2,1)S(1)} %bitcast.61, f32[128,1,128]{2,1,0:T(1,128)S(1)} %pad.4.gate_ref), custom_call_target="tpu_custom_call" | custom-call | tf_op jit(solution)/shard_map/pallas_call | solution.py:172
  161.6 0.1 multiply_convert_fusion.2
  161.7 0.7 copy.16
  162.4 1.3 fusion.9
  163.7 0.0 reduce-scatter.5.cloned.1.call-done
  163.7 3.3 %convert_bitcast_fusion = bf16[1,384,2048]{2,1,0:T(8,128)(2,1)} fusion(f32[384,2048]{1,0:T(8,128)} %reduce-scatter.5.cloned.1.call-done), kind=kLoop, calls=%fused_computation.17 | loop fusion | flops 786432 | bytes 4718592 | tf_op jit(solution)/shard_map/broadcast_in_dim | solution.py:194
  166.9 0.0 reduce-scatter.3.cloned.1.call-done
  166.9 3.2 %convert_bitcast_fusion.1 = bf16[1,2048,384]{2,1,0:T(8,128)(2,1)} fusion(f32[2048,384]{1,0:T(8,128)} %reduce-scatter.3.cloned.1.call-done), kind=kLoop, calls=%fused_computation.18 | loop fusion | flops 786432 | bytes 4718592 | tf_op jit(solution)/shard_map/broadcast_in_dim | solution.py:193
  (2 shorter events, 0.1 us)
Async XLA Ops:
  7.2 1.6 copy-start.4
  7.2 1.9 %copy-start.6 = (bf16[1,1,128,3]{2,3,1,0:T(4,128)(2,1)S(1)}, bf16[1,1,128,3]{2,3,1,0:T(4,128)(2,1)}, u32[]{:S(2)}) copy-start(bf16[1,1,128,3]{2,3,1,0:T(4,128)(2,1)} %param.9) | copy-start | bytes 2308
  7.2 2.2 %copy-start.5 = (s32[1,1,128,3]{2,1,3,0:T(1,128)S(1)}, s32[1,1,128,3]{2,1,3,0:T(1,128)}, u32[]{:S(2)}) copy-start(s32[1,1,128,3]{2,1,3,0:T(1,128)} %param.10) | copy-start | bytes 4612
  7.2 2.6 %copy-start.2 = (bf16[1,128,2048]{2,1,0:T(8,128)(2,1)S(1)}, bf16[1,128,2048]{2,1,0:T(8,128)(2,1)}, u32[]{:S(2)}) copy-start(bf16[1,128,2048]{2,1,0:T(8,128)(2,1)} %param.7) | copy-start | bytes 1572868
  7.2 85.3 %all-gather.7.cloned.1.call-start = ((), (), s32[]{:S(2)}) async-start(), calls=%async_computation.5 | async-start | bytes 4718592 | tf_op jit(solution)/shard_map/all_gather | solution.py:149
  7.9 1.9 %copy-start.3 = (bf16[1,128,2048]{2,1,0:T(8,128)(2,1)S(1)}, bf16[1,128,2048]{2,1,0:T(8,128)(2,1)}, u32[]{:S(2)}) copy-start(bf16[1,128,2048]{2,1,0:T(8,128)(2,1)} %param.8) | copy-start | bytes 1572868
  8.0 93.6 %all-gather.5.cloned.1.call-start = ((), (), s32[]{:S(2)}) async-start(), calls=%async_computation.4 | async-start | bytes 4718592 | tf_op jit(solution)/shard_map/all_gather | solution.py:150
  8.7 155.0 %reduce-scatter.5.cloned.1.call-start = ((), (), s32[]{:S(2)}) async-start(), calls=%async_computation.3 | async-start | bytes 9437184 | tf_op jit(solution)/shard_map/reduce_scatter | solution.py:169
  95.8 1.0 copy-start.7
  101.4 65.5 %reduce-scatter.3.cloned.1.call-start = ((), (), s32[]{:S(2)}) async-start(), calls=%async_computation.2 | async-start | bytes 9437184 | tf_op jit(solution)/shard_map/reduce_scatter | solution.py:168
  105.5 0.8 copy-start
  110.8 1.1 copy-start.1
Sparse Core Ops, SparseCore 0:
  9.8 19.9 all-gather.6
  31.7 18.7 all-gather.4
  101.6 19.4 reduce-scatter.4
  123.6 21.0 reduce-scatter.2

commit v2 on v0

v2 whole, which is shorter than its diff:
```python
import jax
import jax.numpy as jnp
from jax import lax
from jax.experimental import pallas as pl
from jax.experimental.pallas import tpu as pltpu
from jax.sharding import PartitionSpec as P

MESH = pl.DeviceIdType.MESH
NX, NY, NZ = 4, 4, 8
N = NX * NY * NZ
CHUNKS = NX
PEERS = NY * NZ
LANES = 128
SUB = 16
WIDE = SUB * LANES


def place(me):
    return me % NX, (me // NX) % NY, me // (NX * NY)


def block_of(q, z, y):
    return q * PEERS + z * NY + y


def expert_of(q, z, y):
    return (z * NY + y) * NX + lax.rem(q - y + NX, NX)


def hop(i):
    return lax.rem(i, NZ), lax.div(i, NZ)


def bf16(v):
    return v.astype(jnp.bfloat16)


def dot(a, b, dims=((1,), (0,))):
    return lax.dot_general(a, b, (dims, ((), ())), preferred_element_type=jnp.float32)


def local_wait(ref, sem):
    pltpu.make_async_copy(ref, ref, sem).wait()


def kernel(
    idx_ref, scale_ref, pick_ref, tok_ref, grad_ref, up_ref, down_ref,
    dtok_ref, gback_ref, dup_ref, ddown_ref,
    send, recv, wu, wd, rows_x, rows_g, act, dhid, drow, dsend, back, gsend,
    up_out, up_in, down_out, down_in, total, perm,
    w_sem, f_send, f_recv, r_send, r_recv, g_send, g_recv, d_send, d_recv,
):
    me = lax.axis_index("expert")
    core = lax.axis_index("dp")
    x, y, z = place(me)
    q_me = lax.rem(x + y, NX)
    slots = send.shape[2]
    per_chunk = PEERS * slots
    half = up_ref.shape[1]
    mine = pl.ds(pl.multiple_of(core * half, LANES), half)
    theirs = pl.ds(pl.multiple_of((1 - core) * half, LANES), half)
    partner = {"dp": 1 - core}

    barrier = pltpu.get_barrier_semaphore()
    pl.semaphore_signal(barrier, inc=1, device_id=partner, device_id_type=MESH)

    def greet(step, carry):
        pl.semaphore_signal(
            barrier, inc=1, device_id={"expert": lax.rem(me + step, N)}, device_id_type=MESH
        )
        return carry

    lax.fori_loop(1, N, greet, 0)

    own_up = pltpu.make_async_copy(up_ref, wu.at[:, mine], w_sem.at[0])
    own_up.start()
    own_down = pltpu.make_async_copy(down_ref, wd.at[mine, :], w_sem.at[1])
    own_down.start()

    a = lax.broadcasted_iota(jnp.int32, (SUB * SUB, SUB * SUB), 0)
    b = lax.broadcasted_iota(jnp.int32, (SUB * SUB, SUB * SUB), 1)
    swap = (lax.rem(a, SUB) == lax.div(b, SUB)) & (lax.div(a, SUB) == lax.rem(b, SUB))
    perm[...] = jnp.where(swap, 1.0, 0.0).astype(jnp.bfloat16)

    def fill(target, carry):
        for k in range(slots):
            row = idx_ref[target * slots + k]
            send[target, 0, k] = tok_ref[row]
            scaled = grad_ref[row].astype(jnp.float32) * scale_ref[target * slots + k]
            send[target, 1, k] = bf16(scaled)
        return carry

    lax.fori_loop(0, N, fill, 0)
    pl.semaphore_wait(barrier, N)

    up_copy = pltpu.make_async_remote_copy(
        src_ref=up_ref, dst_ref=wu.at[:, mine], send_sem=w_sem.at[2], recv_sem=w_sem.at[3],
        device_id=partner, device_id_type=MESH,
    )
    up_copy.start()
    down_copy = pltpu.make_async_remote_copy(
        src_ref=down_ref, dst_ref=wd.at[mine, :], send_sem=w_sem.at[4], recv_sem=w_sem.at[5],
        device_id=partner, device_id_type=MESH,
    )
    down_copy.start()

    my_rows = pl.ds(block_of(q_me, z, y) * slots, slots)
    pltpu.make_async_copy(send.at[me], recv.at[:, my_rows], f_recv.at[0]).start()

    def push(n, carry):
        c = lax.div(n, PEERS)
        dz, dy = hop(lax.rem(n, PEERS))
        target = expert_of(lax.rem(q_me + c, NX), lax.rem(z + dz, NZ), lax.rem(y + dy, NY))
        pltpu.make_async_remote_copy(
            src_ref=send.at[target], dst_ref=recv.at[:, my_rows],
            send_sem=f_send, recv_sem=f_recv.at[c],
            device_id={"expert": target}, device_id_type=MESH,
        ).start()
        return carry

    lax.fori_loop(1, N, push, 0)

    own_up.wait()
    own_down.wait()
    up_copy.wait()
    down_copy.wait()

    groups = per_chunk // SUB
    grid_a = lax.broadcasted_iota(jnp.int32, (PEERS, per_chunk), 0)
    grid_b = lax.broadcasted_iota(jnp.int32, (PEERS, per_chunk), 1)
    to_peer = jnp.where(lax.div(grid_b, slots) == grid_a, 1.0, 0.0)
    row_id = lax.broadcasted_iota(jnp.int32, (per_chunk, LANES), 0)
    lane_id = lax.broadcasted_iota(jnp.int32, (per_chunk, LANES), 1)
    to_lane = jnp.where(lax.rem(row_id, slots) == lane_id, 1.0, 0.0)

    def chunk(c, carry):
        q = lax.rem(q_me - c + NX, NX)
        first = pl.multiple_of(q * per_chunk, SUB)
        local_wait(recv.at[:, pl.ds(0, per_chunk)], f_recv.at[c])

        def unpack(g, inner):
            r = pl.ds(pl.multiple_of(first + g * SUB, SUB), SUB)
            both = jnp.concatenate(
                [recv[0, r].reshape(SUB * SUB, LANES), recv[1, r].reshape(SUB * SUB, LANES)], axis=1
            )
            out = bf16(dot(perm[...], both))
            for f in range(SUB):
                part = out[f * SUB : (f + 1) * SUB]
                rows_x[r, f * LANES : (f + 1) * LANES] = part[:, :LANES]
                rows_g[r, f * LANES : (f + 1) * LANES] = part[:, LANES:]
            return inner

        lax.fori_loop(0, groups, unpack, 0)

        here = pl.ds(first, per_chunk)
        gate = jnp.zeros((per_chunk, 1), jnp.float32)
        for t in range(2 * half // 256):
            cols = slice(t * 256, (t + 1) * 256)
            hidden = dot(rows_x[here, :], wu[:, cols])
            upstream = dot(rows_g[here, :], wd[cols, :], ((1,), (1,)))
            s = jax.nn.sigmoid(hidden)
            activation = bf16(hidden * s)
            act[here, cols] = activation
            dhid[here, cols] = bf16(upstream * (s * (1.0 + hidden * (1.0 - s))))
            gate += jnp.sum(activation.astype(jnp.float32) * upstream, axis=1, keepdims=True)

        for t in range(WIDE // 512):
            cols = slice(t * 512, (t + 1) * 512)
            drow[:, cols] = bf16(dot(dhid[here, :], wu[cols, :], ((1,), (1,))))

        for g in range(0, groups, 2):
            pair = [
                jnp.concatenate(
                    [
                        drow[(g + h) * SUB : (g + h + 1) * SUB, f * LANES : (f + 1) * LANES]
                        for f in range(SUB)
                    ],
                    axis=0,
                )
                for h in range(2)
            ]
            out = bf16(dot(perm[...], jnp.concatenate(pair, axis=1)))
            for h in range(2):
                r = pl.ds(pl.multiple_of(first + (g + h) * SUB, SUB), SUB)
                dsend[r] = out[:, h * LANES : (h + 1) * LANES].reshape(SUB, SUB, LANES)

        @pl.when(c == 0)
        def _():
            pltpu.make_async_copy(dsend.at[my_rows], back.at[my_rows], r_recv.at[0]).start()

        def reply(i, inner):
            dz, dy = hop(i)
            zz, yy = lax.rem(z - dz + NZ, NZ), lax.rem(y - dy + NY, NY)
            source = pl.ds(block_of(q, zz, yy) * slots, slots)
            pltpu.make_async_remote_copy(
                src_ref=dsend.at[source], dst_ref=back.at[my_rows],
                send_sem=r_send, recv_sem=r_recv.at[c],
                device_id={"expert": expert_of(q, zz, yy)}, device_id_type=MESH,
            ).start()
            return inner

        lax.fori_loop(jnp.where(c == 0, 1, 0), PEERS, reply, 0)

        spread = lax.dot_general(
            to_peer, gate * to_lane, (((1,), (0,)), ((), ())),
            precision=lax.Precision.HIGHEST, preferred_element_type=jnp.float32,
        )
        gsend[pl.ds(q * PEERS, PEERS)] = spread.reshape(PEERS, 1, LANES)
        return carry

    lax.fori_loop(0, CHUNKS, chunk, 0)

    pltpu.make_async_copy(gsend.at[block_of(q_me, z, y)], gback_ref.at[me], g_recv).start()

    def reply_gate(n, carry):
        c = lax.div(n, PEERS)
        dz, dy = hop(lax.rem(n, PEERS))
        q, zz, yy = lax.rem(q_me - c + NX, NX), lax.rem(z - dz + NZ, NZ), lax.rem(y - dy + NY, NY)
        pltpu.make_async_remote_copy(
            src_ref=gsend.at[block_of(q, zz, yy)], dst_ref=gback_ref.at[me],
            send_sem=g_send, recv_sem=g_recv,
            device_id={"expert": expert_of(q, zz, yy)}, device_id_type=MESH,
        ).start()
        return carry

    lax.fori_loop(1, N, reply_gate, 0)

    tiles = WIDE // 512
    for t in range(tiles):
        cols = slice(t * 512, (t + 1) * 512)
        up_out[cols, :] = dot(rows_x[:, cols], dhid[:, theirs], ((0,), (0,)))
    up_swap = pltpu.make_async_remote_copy(
        src_ref=up_out, dst_ref=up_in, send_sem=d_send.at[0], recv_sem=d_recv.at[0],
        device_id=partner, device_id_type=MESH,
    )
    up_swap.start()
    for t in range(tiles):
        cols = slice(t * 512, (t + 1) * 512)
        down_out[:, cols] = dot(act[:, theirs], rows_g[:, cols], ((0,), (0,)))
    down_swap = pltpu.make_async_remote_copy(
        src_ref=down_out, dst_ref=down_in, send_sem=d_send.at[1], recv_sem=d_recv.at[1],
        device_id=partner, device_id_type=MESH,
    )
    down_swap.start()
    up_swap.wait()
    for t in range(tiles):
        cols = slice(t * 512, (t + 1) * 512)
        both = dot(rows_x[:, cols], dhid[:, mine], ((0,), (0,))) + up_in[cols, :]
        dup_ref[cols, :] = bf16(both)
    down_swap.wait()
    for t in range(tiles):
        cols = slice(t * 512, (t + 1) * 512)
        both = dot(act[:, mine], rows_g[:, cols], ((0,), (0,))) + down_in[:, cols]
        ddown_ref[:, cols] = bf16(both)

    total[...] = jnp.zeros_like(total)

    def combine(c, carry):
        q = lax.rem(q_me + c, NX)
        first = pl.multiple_of(q * per_chunk, SUB)
        local_wait(back.at[pl.ds(0, per_chunk)], r_recv.at[c])
        for g in range(0, groups, 2):
            pair = [
                back[pl.ds(pl.multiple_of(first + (g + h) * SUB, SUB), SUB)].reshape(SUB * SUB, LANES)
                for h in range(2)
            ]
            out = bf16(dot(perm[...], jnp.concatenate(pair, axis=1)))
            for h in range(2):
                for f in range(SUB):
                    drow[(g + h) * SUB : (g + h + 1) * SUB, f * LANES : (f + 1) * LANES] = out[
                        f * SUB : (f + 1) * SUB, h * LANES : (h + 1) * LANES
                    ]
        token = lax.broadcasted_iota(jnp.int32, (total.shape[0], per_chunk), 0)
        chosen = bf16(jnp.where(token == pick_ref[q], 1.0, 0.0))
        for t in range(tiles):
            cols = slice(t * 512, (t + 1) * 512)
            total[:, cols] += dot(chosen, drow[:, cols])
        return carry

    lax.fori_loop(0, CHUNKS, combine, 0)
    dtok_ref[...] = bf16(total[...])

    local_wait(gback_ref, g_recv)
    local_wait(gsend.at[pl.ds(0, N - 1)], g_send)
    local_wait(send.at[pl.ds(0, N - 1)], f_send)
    local_wait(dsend.at[pl.ds(0, (N - 1) * slots)], r_send)


def per_device(tokens, grad_out, gates, slot_index, slot_count, up_weight, down_weight):
    experts, slots = slot_index.shape[2:]
    held, width = tokens.shape[1:]
    half = up_weight.shape[2]
    total = experts * slots
    picks = slot_index[0, 0]
    live = lax.broadcasted_iota(jnp.int32, (experts, slots), 1) < slot_count[0, 0][:, None]
    scale = jnp.where(live, gates[0, 0].astype(jnp.float32), 0.0)
    cube = picks.reshape(NZ, NY, NX, slots)
    order = jnp.stack([jnp.roll(cube[:, j], j, axis=1) for j in range(NY)], axis=1)
    order = jnp.transpose(order, (2, 0, 1, 3)).reshape(CHUNKS, 1, PEERS * slots)

    vmem = pl.BlockSpec(memory_space=pltpu.VMEM)
    smem = pl.BlockSpec(memory_space=pltpu.SMEM)
    anywhere = pl.BlockSpec(memory_space=pl.ANY)
    low, full = jnp.bfloat16, jnp.float32
    dma = pltpu.SemaphoreType.DMA
    d_tokens, gate_back, d_up, d_down = pl.pallas_call(
        kernel,
        out_shape=(
            jax.ShapeDtypeStruct((held, width), low),
            jax.ShapeDtypeStruct((experts, 1, LANES), full),
            jax.ShapeDtypeStruct((width, half), low),
            jax.ShapeDtypeStruct((half, width), low),
        ),
        in_specs=[smem, smem, vmem, vmem, vmem, anywhere, anywhere],
        out_specs=(vmem, vmem, vmem, vmem),
        scratch_shapes=[
            pltpu.VMEM((experts, 2, slots, SUB, LANES), low),
            pltpu.VMEM((2, total, SUB, LANES), low),
            pltpu.VMEM((width, 2 * half), low),
            pltpu.VMEM((2 * half, width), low),
            pltpu.VMEM((total, width), low),
            pltpu.VMEM((total, width), low),
            pltpu.VMEM((total, 2 * half), low),
            pltpu.VMEM((total, 2 * half), low),
            pltpu.VMEM((PEERS * slots, width), low),
            pltpu.VMEM((total, SUB, LANES), low),
            pltpu.VMEM((total, SUB, LANES), low),
            pltpu.VMEM((experts, 1, LANES), full),
            pltpu.VMEM((width, half), full),
            pltpu.VMEM((width, half), full),
            pltpu.VMEM((half, width), full),
            pltpu.VMEM((half, width), full),
            pltpu.VMEM((held, width), full),
            pltpu.VMEM((SUB * SUB, SUB * SUB), low),
            dma((6,)),
            dma,
            dma((CHUNKS,)),
            dma,
            dma((CHUNKS,)),
            dma,
            dma,
            dma((2,)),
            dma((2,)),
        ],
        compiler_params=pltpu.CompilerParams(
            collective_id=0, has_side_effects=True, vmem_limit_bytes=56 << 20
        ),
    )(
        picks.reshape(total),
        scale.reshape(total),
        order,
        tokens[0].reshape(held, SUB, LANES),
        grad_out[0].reshape(held, SUB, LANES),
        up_weight[0],
        down_weight[0],
    )
    inverse = jnp.where(live, 1.0 / jnp.where(live, scale, 1.0), 0.0)
    d_gates = gate_back[:, 0, :slots] * inverse
    return (
        d_tokens[None],
        d_gates.astype(low)[None, None],
        d_up[None],
        d_down[None],
    )


def solution(mesh):
    in_specs = (
        P("dp", "expert", None),
        P("dp", "expert", None),
        P("dp", "expert", None, None),
        P("dp", "expert", None, None),
        P("dp", "expert", None),
        P("expert", None, "dp"),
        P("expert", "dp", None),
    )
    out_specs = (
        P("dp", "expert", None),
        P("dp", "expert", None, None),
        P("expert", None, "dp"),
        P("expert", "dp", None),
    )
    return jax.shard_map(
        per_device, mesh=mesh, in_specs=in_specs, out_specs=out_specs, check_vma=False
    )
```

time: 307 us -> 139 us (0.45)
  waiting for transfers between devices: 161 us -> 0 us
  Pallas kernels: 0 us -> 121 us
  starting transfers between devices: 54.5 us -> 0 us
  matrix products: 27.3 us -> 0 us
  local copies, waits for them, and re-layouts: 30.7 us -> 14 us
  other arithmetic: 19.2 us -> 3.12 us
  between operations: 13.9 us -> 0.71 us
    all_to_all x6 -> x0, waiting for transfers between devices: 159 us -> none  [the longest x1 50.3 us: per_device(): lax.all_to_all(d_rows.astype(jnp.bfloat16), 'expert', split_axis=0, conca...]
    pallas_call x0 -> x1, Pallas kernels: none -> 121 us  [per_device(): pl.pallas_call(kernel, out_shape=(jax.ShapeDtypeStruct((held, width), low...]
    all_to_all x6 -> x0, starting transfers between devices: 54.1 us -> none  [the longest x1 15 us: per_device(): lax.all_to_all(live, 'expert', split_axis=0, concat_axis=0, tiled=True)]
    dot_general x6 -> x0, matrix products: 27.3 us -> none  [the longest x1 6.71 us: expert_backward(): lax.dot_general(scaled, rows_grad, (((0,), (0,)), ((), ())), preferred_el...]
    reshape x4 -> x1, local copies, waits for them, and re-layouts: 13.9 us -> 0.72 us  [per_device(): order = jnp.transpose(order, (2, 0, 1, 3)).reshape(CHUNKS, 1, PEERS * slots)]
    unnamed x9 -> x14, local copies, waits for them, and re-layouts: 2.14 us -> 11 us
    broadcast_in_dim x3 -> x0, other arithmetic: 7.33 us -> none  [the longest x1 3.27 us: per_device(): d_down.astype(jnp.bfloat16)[None]]
    scatter-add x1 -> x0, other arithmetic: 6.85 us -> none  [per_device(): summed = jnp.zeros((own_tokens.shape[0], width), jnp.float32).at[flat].ad...]
  transfers between devices with their start and end apart: 10 -> 0, of which waited for: 6 -> 0; matrix products, arithmetic and copies ran while one was open for 19% -> 0% of each run, Pallas kernels for 0% -> 0%
where the time goes in v2:
time: 139 us
  Pallas kernels  121 us (87%)
  local copies, waits for them, and re-layouts  14 us (10%)
  other arithmetic  3.12 us (2%)
    pallas_call x1, Pallas kernels, per_device(): pl.pallas_call(kernel, out_shape=(jax.ShapeDtypeStruct((held, width), low...  121 us
    unnamed x14, local copies, waits for them, and re-layouts  11 us

profile of v2, /device:TPU:32, one launch (start us, length us, event | category | flops | bytes accessed | tf_op | source)
XLA Modules:
  0.0 139.2 jit_solution(8281916105227101843)
XLA Ops:
  0.6 0.0 copy-start.1
  0.6 0.8 reduce
  1.4 0.7 iota_compare_fusion.1
  2.1 0.2 lt.28
  2.4 0.8 copy.15
  3.2 0.2 reshape.52
  3.4 0.6 broadcast_select_fusion.scale_ref
  4.0 0.1 reshape_squeeze.13
  4.2 0.1 copy.18
  4.3 0.1 copy.21
  4.4 0.1 copy.17
  4.5 0.1 copy.20
  4.6 0.1 copy.16
  4.7 0.1 copy.19
  4.8 0.1 add_bitcast_fusion
  4.8 0.3 copy.22
  5.2 0.7 reshape.51
  5.9 0.8 copy.14
  6.7 0.8 reshape_squeeze.12.idx_ref
  7.5 1.9 %copy.25 = bf16[16,8,16,128]{3,2,1,0:T(8,128)(2,1)} copy(bf16[16,8,16,128]{3,1,2,0:T(8,128)(2,1)} %bitcast.39) | data formatting | bytes 1048576
  9.4 0.0 copy-done.1
  9.4 0.9 copy.26
  10.3 0.0 copy-start.2
  10.3 121.4 %shard_map.102 = (bf16[128,2048]{1,0:T(8,128)(2,1)}, f32[128,1,128]{2,1,0:T(1,128)}, bf16[2048,384]{1,0:T(8,128)(2,1)}, bf16[384,2048]{1,0:T(8,128)(2,1)}) custom-call(s32[384]{0:T(512)} %reshape_squeeze.12.idx_ref, f32[384]{0:T(512)} %broadcast_select_fusion.scale_ref, s32[4,1,96]{2,1,0:T(1,128)} %bitcast.48, bf16[128,16,128]{2,1,0:T(8,128)(2,1)} %bitcast.33, ...), custom_call_target="tpu_custom_call" | custom-call | tf_op jit(solution)/shard_map/pallas_call | solution.py:306
  131.7 0.0 copy-done.2
  131.7 0.9 fusion.3
  132.7 0.7 copy.24
  133.3 1.9 %copy.30 = bf16[1,128,2048]{2,1,0:T(8,128)(2,1)} copy(bf16[1,128,2048]{2,1,0:T(8,128)(2,1)} %bitcast.41) | data formatting | bytes 1048576
  135.2 0.0 copy-start
  135.2 2.8 %copy.31 = bf16[1,2048,384]{2,1,0:T(8,128)(2,1)} copy(bf16[1,2048,384]{2,1,0:T(8,128)(2,1)} %bitcast.38) | data formatting | bytes 3145728
  138.0 0.0 copy-done
  138.0 1.1 copy.32
  (8 shorter events, 0.1 us)
Async XLA Ops:
  0.6 8.8 %copy-start.1 = (bf16[1,128,2048]{2,1,0:T(8,128)(2,1)S(1)}, bf16[1,128,2048]{2,1,0:T(8,128)(2,1)}, u32[]{:S(2)}) copy-start(bf16[1,128,2048]{2,1,0:T(8,128)(2,1)} %param.8) | copy-start | bytes 1572868
  10.3 121.4 %copy-start.2 = (s32[1,1,128]{2,1,0:T(1,128)S(1)}, s32[1,1,128]{2,1,0:T(1,128)}, u32[]{:S(2)}) copy-start(s32[1,1,128]{2,1,0:T(1,128)} %param.11) | copy-start | bytes 1540
  135.2 2.8 %copy-start = (bf16[384,2048]{1,0:T(8,128)(2,1)S(1)}, bf16[384,2048]{1,0:T(8,128)(2,1)}, u32[]{:S(2)}) copy-start(bf16[384,2048]{1,0:T(8,128)(2,1)} %get-tuple-element.11) | copy-start | bytes 4718596

commit v3 on v2

--- a/solution.py
+++ b/solution.py
@@ -44,11 +44,12 @@
 
 
 def kernel(
-    idx_ref, scale_ref, pick_ref, tok_ref, grad_ref, up_ref, down_ref,
-    dtok_ref, gback_ref, dup_ref, ddown_ref,
+    idx_ref, pick_ref, gates_ref, count_ref, tok_ref, grad_ref, up_ref, down_ref,
+    dtok_ref, dgate_ref, dup_ref, ddown_ref,
+    tok, grad, scale_vec, scale, gback,
     send, recv, wu, wd, rows_x, rows_g, act, dhid, drow, dsend, back, gsend,
     up_out, up_in, down_out, down_in, total, perm,
-    w_sem, f_send, f_recv, r_send, r_recv, g_send, g_recv, d_send, d_recv,
+    w_sem, s_sem, f_send, f_recv, r_send, r_recv, g_send, g_recv, d_send, d_recv,
 ):
     me = lax.axis_index("expert")
     core = lax.axis_index("dp")
@@ -82,15 +83,38 @@
     swap = (lax.rem(a, SUB) == lax.div(b, SUB)) & (lax.div(a, SUB) == lax.rem(b, SUB))
     perm[...] = jnp.where(swap, 1.0, 0.0).astype(jnp.bfloat16)
 
-    def fill(target, carry):
+    scale_vec[...] = jnp.zeros_like(scale_vec)
+    for k in range(slots):
+        live = jnp.where(count_ref[...] > k, 1.0, 0.0)
+        scale_vec[k : k + 1, :] = live * gates_ref[k : k + 1, :].astype(jnp.float32)
+    to_scalars = pltpu.make_async_copy(scale_vec, scale, s_sem)
+    to_scalars.start()
+
+    def by_row(g, carry):
+        r = pl.ds(pl.multiple_of(g * SUB, SUB), SUB)
+        both = jnp.concatenate(
+            [
+                jnp.concatenate(
+                    [ref[r, f * LANES : (f + 1) * LANES] for f in range(SUB)], axis=0
+                )
+                for ref in (tok_ref, grad_ref)
+            ],
+            axis=1,
+        )
+        out = bf16(dot(perm[...], both))
+        tok[r] = out[:, :LANES].reshape(SUB, SUB, LANES)
+        grad[r] = out[:, LANES:].reshape(SUB, SUB, LANES)
+        return carry
+
+    lax.fori_loop(0, tok.shape[0] // SUB, by_row, 0)
+    to_scalars.wait()
+
+    def fill(target):
         for k in range(slots):
-            row = idx_ref[target * slots + k]
-            send[target, 0, k] = tok_ref[row]
-            scaled = grad_ref[row].astype(jnp.float32) * scale_ref[target * slots + k]
-            send[target, 1, k] = bf16(scaled)
-        return carry
-
-    lax.fori_loop(0, N, fill, 0)
+            row = idx_ref[k, 0, target]
+            send[target, 0, k] = tok[row]
+            send[target, 1, k] = bf16(grad[row].astype(jnp.float32) * scale[k, target])
+
     pl.semaphore_wait(barrier, N)
 
     up_copy = pltpu.make_async_remote_copy(
@@ -105,12 +129,12 @@
     down_copy.start()
 
     my_rows = pl.ds(block_of(q_me, z, y) * slots, slots)
-    pltpu.make_async_copy(send.at[me], recv.at[:, my_rows], f_recv.at[0]).start()
 
     def push(n, carry):
         c = lax.div(n, PEERS)
         dz, dy = hop(lax.rem(n, PEERS))
         target = expert_of(lax.rem(q_me + c, NX), lax.rem(z + dz, NZ), lax.rem(y + dy, NY))
+        fill(target)
         pltpu.make_async_remote_copy(
             src_ref=send.at[target], dst_ref=recv.at[:, my_rows],
             send_sem=f_send, recv_sem=f_recv.at[c],
@@ -119,6 +143,8 @@
         return carry
 
     lax.fori_loop(1, N, push, 0)
+    fill(me)
+    pltpu.make_async_copy(send.at[me], recv.at[:, my_rows], f_recv.at[0]).start()
 
     own_up.wait()
     own_down.wait()
@@ -210,14 +236,14 @@
 
     lax.fori_loop(0, CHUNKS, chunk, 0)
 
-    pltpu.make_async_copy(gsend.at[block_of(q_me, z, y)], gback_ref.at[me], g_recv).start()
+    pltpu.make_async_copy(gsend.at[block_of(q_me, z, y)], gback.at[me], g_recv).start()
 
     def reply_gate(n, carry):
         c = lax.div(n, PEERS)
         dz, dy = hop(lax.rem(n, PEERS))
         q, zz, yy = lax.rem(q_me - c + NX, NX), lax.rem(z - dz + NZ, NZ), lax.rem(y - dy + NY, NY)
         pltpu.make_async_remote_copy(
-            src_ref=gsend.at[block_of(q, zz, yy)], dst_ref=gback_ref.at[me],
+            src_ref=gsend.at[block_of(q, zz, yy)], dst_ref=gback.at[me],
             send_sem=g_send, recv_sem=g_recv,
             device_id={"expert": expert_of(q, zz, yy)}, device_id_type=MESH,
         ).start()
@@ -270,8 +296,16 @@
                     drow[(g + h) * SUB : (g + h + 1) * SUB, f * LANES : (f + 1) * LANES] = out[
                         f * SUB : (f + 1) * SUB, h * LANES : (h + 1) * LANES
                     ]
+        expert = lax.broadcasted_iota(jnp.int32, (N, per_chunk), 0)
+        peer = lax.div(lax.broadcasted_iota(jnp.int32, (N, per_chunk), 1), slots)
+        owner = expert_of(q, lax.div(peer, NY), lax.rem(peer, NY))
+        owned = jnp.where(expert == owner, 1.0, 0.0)
+        slot = lax.rem(lax.broadcasted_iota(jnp.int32, (1, per_chunk), 1), slots)
+        picked = jnp.zeros((1, per_chunk), jnp.float32)
+        for k in range(slots):
+            picked += jnp.where(slot == k, dot(pick_ref[k].astype(jnp.float32), owned), 0.0)
         token = lax.broadcasted_iota(jnp.int32, (total.shape[0], per_chunk), 0)
-        chosen = bf16(jnp.where(token == pick_ref[q], 1.0, 0.0))
+        chosen = bf16(jnp.where(token.astype(jnp.float32) == picked, 1.0, 0.0))
         for t in range(tiles):
             cols = slice(t * 512, (t + 1) * 512)
             total[:, cols] += dot(chosen, drow[:, cols])
@@ -280,10 +314,35 @@
     lax.fori_loop(0, CHUNKS, combine, 0)
     dtok_ref[...] = bf16(total[...])
 
-    local_wait(gback_ref, g_recv)
+    local_wait(gback, g_recv)
+    eye = jnp.where(
+        lax.broadcasted_iota(jnp.int32, (8, LANES), 0)
+        == lax.broadcasted_iota(jnp.int32, (8, LANES), 1),
+        1.0,
+        0.0,
+    )
+    by_slot = lax.dot_general(
+        eye, gback[...].reshape(N, LANES), (((1,), (1,)), ((), ())),
+        precision=lax.Precision.HIGHEST, preferred_element_type=jnp.float32,
+    )
+    for k in range(slots):
+        c = scale_vec[k : k + 1, :]
+        inverse = jnp.where(c > 0.0, 1.0 / jnp.where(c > 0.0, c, 1.0), 0.0)
+        dgate_ref[k : k + 1, :] = bf16(by_slot[k : k + 1, :] * inverse)
     local_wait(gsend.at[pl.ds(0, N - 1)], g_send)
     local_wait(send.at[pl.ds(0, N - 1)], f_send)
     local_wait(dsend.at[pl.ds(0, (N - 1) * slots)], r_send)
+
+
+def write_out(*refs):
+    count = len(refs) // 2
+    copies = [
+        pltpu.make_async_copy(refs[i], refs[count + i], refs[-1].at[i]) for i in range(count)
+    ]
+    for copy in copies:
+        copy.start()
+    for copy in copies:
+        copy.wait()
 
 
 def per_device(tokens, grad_out, gates, slot_index, slot_count, up_weight, down_weight):
@@ -291,29 +350,25 @@
     held, width = tokens.shape[1:]
     half = up_weight.shape[2]
     total = experts * slots
-    picks = slot_index[0, 0]
-    live = lax.broadcasted_iota(jnp.int32, (experts, slots), 1) < slot_count[0, 0][:, None]
-    scale = jnp.where(live, gates[0, 0].astype(jnp.float32), 0.0)
-    cube = picks.reshape(NZ, NY, NX, slots)
-    order = jnp.stack([jnp.roll(cube[:, j], j, axis=1) for j in range(NY)], axis=1)
-    order = jnp.transpose(order, (2, 0, 1, 3)).reshape(CHUNKS, 1, PEERS * slots)
+    picks = slot_index[0, 0].T.reshape(slots, 1, experts)
 
     vmem = pl.BlockSpec(memory_space=pltpu.VMEM)
     smem = pl.BlockSpec(memory_space=pltpu.SMEM)
     anywhere = pl.BlockSpec(memory_space=pl.ANY)
     low, full = jnp.bfloat16, jnp.float32
     dma = pltpu.SemaphoreType.DMA
-    d_tokens, gate_back, d_up, d_down = pl.pallas_call(
+    outs = (((held, width), low), ((slots, experts), low), ((width, half), low), ((half, width), low))
+    results = pl.pallas_call(
         kernel,
-        out_shape=(
-            jax.ShapeDtypeStruct((held, width), low),
-            jax.ShapeDtypeStruct((experts, 1, LANES), full),
-            jax.ShapeDtypeStruct((width, half), low),
-            jax.ShapeDtypeStruct((half, width), low),
-        ),
-        in_specs=[smem, smem, vmem, vmem, vmem, anywhere, anywhere],
+        out_shape=tuple(pltpu.VMEM(shape, dtype) for shape, dtype in outs),
+        in_specs=[smem, vmem, vmem, vmem, vmem, vmem, anywhere, anywhere],
         out_specs=(vmem, vmem, vmem, vmem),
         scratch_shapes=[
+            pltpu.VMEM((held, SUB, LANES), low),
+            pltpu.VMEM((held, SUB, LANES), low),
+            pltpu.VMEM((8, experts), full),
+            pltpu.SMEM((8, experts), full),
+            pltpu.VMEM((experts, 1, LANES), full),
             pltpu.VMEM((experts, 2, slots, SUB, LANES), low),
             pltpu.VMEM((2, total, SUB, LANES), low),
             pltpu.VMEM((width, 2 * half), low),
@@ -334,6 +389,7 @@
             pltpu.VMEM((SUB * SUB, SUB * SUB), low),
             dma((6,)),
             dma,
+            dma,
             dma((CHUNKS,)),
             dma,
             dma((CHUNKS,)),
@@ -343,25 +399,26 @@
             dma((2,)),
         ],
         compiler_params=pltpu.CompilerParams(
-            collective_id=0, has_side_effects=True, vmem_limit_bytes=56 << 20
+            collective_id=0, has_side_effects=True, vmem_limit_bytes=50 << 20
         ),
     )(
-        picks.reshape(total),
-        scale.reshape(total),
-        order,
-        tokens[0].reshape(held, SUB, LANES),
-        grad_out[0].reshape(held, SUB, LANES),
+        picks,
+        picks,
+        gates[0, 0].T,
+        slot_count[0],
+        tokens[0],
+        grad_out[0],
         up_weight[0],
         down_weight[0],
     )
-    inverse = jnp.where(live, 1.0 / jnp.where(live, scale, 1.0), 0.0)
-    d_gates = gate_back[:, 0, :slots] * inverse
-    return (
-        d_tokens[None],
-        d_gates.astype(low)[None, None],
-        d_up[None],
-        d_down[None],
-    )
+    d_tokens, d_gate, d_up, d_down = pl.pallas_call(
+        write_out,
+        out_shape=tuple(jax.ShapeDtypeStruct(shape, dtype) for shape, dtype in outs),
+        in_specs=[vmem] * 4,
+        out_specs=(anywhere,) * 4,
+        scratch_shapes=[dma((4,))],
+    )(*results)
+    return d_tokens[None], d_gate.T[None, None], d_up[None], d_down[None]
 
 
 def solution(mesh):

time: 139 us -> 130 us (0.935)
  local copies, waits for them, and re-layouts: 14 us -> 5.66 us
  other arithmetic: 3.12 us -> 0 us
  Pallas kernels: 121 us -> 124 us
    unnamed x14 -> x13, local copies, waits for them, and re-layouts: 11 us -> 5.66 us
    pallas_call x1 -> x2, Pallas kernels: 121 us -> 124 us  [the longest x1 120 us: per_device(): pl.pallas_call(kernel, out_shape=tuple((pltpu.VMEM(shape, dtype) for shap...]
where the time goes in v3:
time: 130 us
  Pallas kernels  124 us (95%)
  local copies, waits for them, and re-layouts  5.66 us (4%)
    pallas_call x1, Pallas kernels, per_device(): pl.pallas_call(kernel, out_shape=tuple((pltpu.VMEM(shape, dtype) for shap...  120 us
    unnamed x13, local copies, waits for them, and re-layouts  5.66 us
    pallas_call x1, Pallas kernels, per_device(): pl.pallas_call(write_out, out_shape=tuple((jax.ShapeDtypeStruct(shape, dt...  3.92 us

profile of v3, /device:TPU:32, one launch (start us, length us, event | category | flops | bytes accessed | tf_op | source)
XLA Modules:
  0.0 130.1 jit_solution(1731415314607713936)
XLA Ops:
  0.6 0.7 copy.13
  1.3 0.0 copy-start.3
  1.3 0.7 copy-done.3
  2.0 0.0 copy-start.5
  2.0 0.7 copy-done.5
  2.7 119.9 %shard_map.102 = (bf16[128,2048]{1,0:T(8,128)(2,1)S(1)}, bf16[3,128]{1,0:T(4,128)(2,1)S(1)}, bf16[2048,384]{1,0:T(8,128)(2,1)S(1)}, bf16[384,2048]{1,0:T(8,128)(2,1)S(1)}) custom-call(s32[3,1,128]{2,1,0:T(1,128)S(1)} %reshape.11.idx_ref.pick_ref, s32[3,1,128]{2,1,0:T(1,128)S(1)} %reshape.11.idx_ref.pick_ref, bf16[3,128]{1,0:T(4,128)(2,1)S(1)} %bitcast.19, ...), custom_call_target="tpu_custom_call" | custom-call | tf_op jit(solution)/shard_map/pallas_call | solution.py:361
  122.5 0.0 copy-start
  122.5 1.1 copy-done
  123.7 0.0 copy-start.1
  123.7 1.2 copy-done.1
  124.8 0.0 copy-start.2
  124.8 0.8 copy-done.2
  125.6 0.0 copy-start.4
  125.6 0.6 copy-done.4
  126.2 3.9 %shard_map.103 = (bf16[128,2048]{1,0:T(8,128)(2,1)}, bf16[3,128]{1,0:T(4,128)(2,1)}, bf16[2048,384]{1,0:T(8,128)(2,1)}, bf16[384,2048]{1,0:T(8,128)(2,1)}) custom-call(bf16[128,2048]{1,0:T(8,128)(2,1)} %copy-done.2, bf16[3,128]{1,0:T(4,128)(2,1)} %copy-done.4, bf16[2048,384]{1,0:T(8,128)(2,1)} %copy-done, bf16[384,2048]{1,0:T(8,128)(2,1)} %copy-done.1), custom_call_target="tpu_custom_call" | custom-call | tf_op jit(solution)/shard_map/pallas_call | solution.py:414
  (1 shorter events, 0.0 us)
Async XLA Ops:
  1.3 0.7 copy-start.3
  2.0 0.7 copy-start.5
  122.5 1.1 copy-start
  123.7 1.2 copy-start.1
  124.8 0.8 copy-start.2
  125.6 0.6 copy-start.4

commit v4 on v3

--- a/solution.py
+++ b/solution.py
@@ -44,12 +44,12 @@
 
 
 def kernel(
-    idx_ref, pick_ref, gates_ref, count_ref, tok_ref, grad_ref, up_ref, down_ref,
+    idx_ref, pick_hbm, gates_hbm, count_hbm, tok_ref, grad_ref, up_ref, down_ref,
     dtok_ref, dgate_ref, dup_ref, ddown_ref,
-    tok, grad, scale_vec, scale, gback,
+    pick_ref, gates_ref, count_ref, tok, grad, scale_vec, scale, gback,
     send, recv, wu, wd, rows_x, rows_g, act, dhid, drow, dsend, back, gsend,
     up_out, up_in, down_out, down_in, total, perm,
-    w_sem, s_sem, f_send, f_recv, r_send, r_recv, g_send, g_recv, d_send, d_recv,
+    w_sem, s_sem, small_sem, f_send, f_recv, r_send, r_recv, g_send, g_recv, d_send, d_recv,
 ):
     me = lax.axis_index("expert")
     core = lax.axis_index("dp")
@@ -78,11 +78,22 @@
     own_down = pltpu.make_async_copy(down_ref, wd.at[mine, :], w_sem.at[1])
     own_down.start()
 
+    small = [
+        pltpu.make_async_copy(src, dst, small_sem.at[i])
+        for i, (src, dst) in enumerate(
+            ((gates_hbm, gates_ref), (count_hbm, count_ref), (pick_hbm, pick_ref))
+        )
+    ]
+    for copy in small:
+        copy.start()
+
     a = lax.broadcasted_iota(jnp.int32, (SUB * SUB, SUB * SUB), 0)
     b = lax.broadcasted_iota(jnp.int32, (SUB * SUB, SUB * SUB), 1)
     swap = (lax.rem(a, SUB) == lax.div(b, SUB)) & (lax.div(a, SUB) == lax.rem(b, SUB))
     perm[...] = jnp.where(swap, 1.0, 0.0).astype(jnp.bfloat16)
 
+    for copy in small:
+        copy.wait()
     scale_vec[...] = jnp.zeros_like(scale_vec)
     for k in range(slots):
         live = jnp.where(count_ref[...] > k, 1.0, 0.0)
@@ -350,20 +361,28 @@
     held, width = tokens.shape[1:]
     half = up_weight.shape[2]
     total = experts * slots
-    picks = slot_index[0, 0].T.reshape(slots, 1, experts)
+    picks = jnp.transpose(slot_index[0], (2, 0, 1))
 
     vmem = pl.BlockSpec(memory_space=pltpu.VMEM)
     smem = pl.BlockSpec(memory_space=pltpu.SMEM)
     anywhere = pl.BlockSpec(memory_space=pl.ANY)
+    hbm = pl.BlockSpec(memory_space=pltpu.HBM)
     low, full = jnp.bfloat16, jnp.float32
+
+    def stay(array):
+        return pltpu.with_memory_space_constraint(array, pltpu.HBM)
+
     dma = pltpu.SemaphoreType.DMA
     outs = (((held, width), low), ((slots, experts), low), ((width, half), low), ((half, width), low))
     results = pl.pallas_call(
         kernel,
         out_shape=tuple(pltpu.VMEM(shape, dtype) for shape, dtype in outs),
-        in_specs=[smem, vmem, vmem, vmem, vmem, vmem, anywhere, anywhere],
+        in_specs=[smem, hbm, hbm, hbm, vmem, vmem, hbm, hbm],
         out_specs=(vmem, vmem, vmem, vmem),
         scratch_shapes=[
+            pltpu.VMEM((slots, 1, experts), jnp.int32),
+            pltpu.VMEM((slots, experts), low),
+            pltpu.VMEM((1, experts), jnp.int32),
             pltpu.VMEM((held, SUB, LANES), low),
             pltpu.VMEM((held, SUB, LANES), low),
             pltpu.VMEM((8, experts), full),
@@ -389,6 +408,7 @@
             pltpu.VMEM((SUB * SUB, SUB * SUB), low),
             dma((6,)),
             dma,
+            dma((3,)),
             dma,
             dma((CHUNKS,)),
             dma,
@@ -403,9 +423,9 @@
         ),
     )(
         picks,
-        picks,
-        gates[0, 0].T,
-        slot_count[0],
+        stay(picks),
+        stay(gates[0, 0].T),
+        stay(slot_count[0]),
         tokens[0],
         grad_out[0],
         up_weight[0],
@@ -417,7 +437,8 @@
         in_specs=[vmem] * 4,
         out_specs=(anywhere,) * 4,
         scratch_shapes=[dma((4,))],
-    )(*results)
+        compiler_params=pltpu.CompilerParams(vmem_limit_bytes=1 << 20),
+    )(*(pltpu.with_memory_space_constraint(r, pltpu.VMEM) for r in results))
     return d_tokens[None], d_gate.T[None, None], d_up[None], d_down[None]
 
 

time: 130 us -> 123 us (0.946)
  local copies, waits for them, and re-layouts: 5.66 us -> 0 us
    unnamed x13 -> x0, local copies, waits for them, and re-layouts: 5.66 us -> none
    pallas_call x1, Pallas kernels: 3.92 us -> 1.87 us  [per_device(): pl.pallas_call(write_out, out_shape=tuple((jax.ShapeDtypeStruct(shape, dt...]
where the time goes in v4:
time: 123 us
  Pallas kernels  123 us (100%)
    pallas_call x1, Pallas kernels, per_device(): pl.pallas_call(kernel, out_shape=tuple((pltpu.VMEM(shape, dtype) for shap...  121 us

profile of v4, /device:TPU:32, one launch (start us, length us, event | category | flops | bytes accessed | tf_op | source)
XLA Modules:
  0.0 123.3 jit_solution(6745175089199121394)
XLA Ops:
  0.6 120.8 %shard_map.102 = (bf16[128,2048]{1,0:T(8,128)(2,1)S(1)}, bf16[3,128]{1,0:T(4,128)(2,1)S(1)}, bf16[2048,384]{1,0:T(8,128)(2,1)S(1)}, bf16[384,2048]{1,0:T(8,128)(2,1)S(1)}) custom-call(s32[3,1,128]{2,1,0:T(1,128)} %bitcast.21, s32[3,1,128]{2,1,0:T(1,128)} %bitcast.22, bf16[3,128]{1,0:T(4,128)(2,1)} %bitcast.23, s32[1,128]{1,0:T(1,128)} %bitcast.24, ...), custom_call_target="tpu_custom_call" | custom-call | tf_op jit(solution)/shard_map/pallas_call | solution.py:377
  121.5 1.9 %shard_map.103 = (bf16[128,2048]{1,0:T(8,128)(2,1)}, bf16[3,128]{1,0:T(4,128)(2,1)}, bf16[2048,384]{1,0:T(8,128)(2,1)}, bf16[384,2048]{1,0:T(8,128)(2,1)}) custom-call(bf16[128,2048]{1,0:T(8,128)(2,1)S(1)} %get-tuple-element.12.refs_0_, bf16[3,128]{1,0:T(4,128)(2,1)S(1)} %get-tuple-element.13.refs_1_, bf16[2048,384]{1,0:T(8,128)(2,1)S(1)} %get-tuple-element.14.refs_2_, ...), custom_call_target="tpu_custom_call" | custom-call | tf_op jit(solution)/shard_map/pallas_call | solution.py:434

commit v5 on v4

--- a/solution.py
+++ b/solution.py
@@ -13,6 +13,11 @@
 LANES = 128
 SUB = 16
 WIDE = SUB * LANES
+PLANE = NX * NY
+PAIRS = PLANE * PLANE
+CAP = 96
+FEW = 64
+PARTS = 2
 
 
 def place(me):
@@ -43,7 +48,7 @@
     pltpu.make_async_copy(ref, ref, sem).wait()
 
 
-def kernel(
+def padded_kernel(
     idx_ref, pick_hbm, gates_hbm, count_hbm, tok_ref, grad_ref, up_ref, down_ref,
     dtok_ref, dgate_ref, dup_ref, ddown_ref,
     pick_ref, gates_ref, count_ref, tok, grad, scale_vec, scale, gback,
@@ -345,6 +350,543 @@
     local_wait(dsend.at[pl.ds(0, (N - 1) * slots)], r_send)
 
 
+def lean_kernel(
+    idx_ref, pick_hbm, gates_hbm, count_hbm, tok_ref, grad_ref, up_ref, down_ref,
+    dtok_ref, dgate_ref, dup_ref, ddown_ref, flag_ref,
+    pick_ref, gates_ref, count_ref, tok, grad, scale_vec, scale, gback,
+    send, recv, wu, wd, rows_x, rows_g, act, dhid, drow, dsend, back, gsend,
+    up_out, up_in, up_own, down_out, down_in, down_own, total, perm, above,
+    third, r1_in, r1, meta1, live3, o2, r2, meta2, got2, o3, o3_out, r3,
+    d3, rr1_in, rr1, ro2, rr2, ro3, ro3_out, d3back, pack_out, pack_in, pack_src, pack_dst, own_pick, flag_in,
+    w_sem, s_sem, small_sem, f_send, f_recv, r_send, r_recv, g_send, g_recv, d_send, d_recv,
+    t_send, t_recv, m_send, m_recv,
+):
+    me = lax.axis_index("expert")
+    core = lax.axis_index("dp")
+    x, y, z = place(me)
+    p = lax.rem(me, PLANE)
+    q_me = lax.rem(x + y, NX)
+    slots = pick_ref.shape[0]
+    direct = send.shape[2]
+    quarter = PEERS * direct
+    per_chunk = recv.shape[1] // PARTS
+    half = up_ref.shape[1]
+    mine = pl.ds(pl.multiple_of(core * half, LANES), half)
+    partner = {"dp": 1 - core}
+    my_lanes = pl.ds(pl.multiple_of(p * LANES, LANES), LANES)
+
+    barrier = pltpu.get_barrier_semaphore()
+    pl.semaphore_signal(barrier, inc=1, device_id=partner, device_id_type=MESH)
+
+    def greet(step, carry):
+        pl.semaphore_signal(
+            barrier, inc=1, device_id={"expert": lax.rem(me + step, N)}, device_id_type=MESH
+        )
+        return carry
+
+    lax.fori_loop(1, N, greet, 0)
+
+    small = [
+        pltpu.make_async_copy(src, dst, small_sem.at[i])
+        for i, (src, dst) in enumerate(
+            ((gates_hbm, gates_ref), (count_hbm, count_ref), (pick_hbm, pick_ref))
+        )
+    ]
+    for copy in small:
+        copy.start()
+    own_up = pltpu.make_async_copy(up_ref, wu.at[:, mine], w_sem.at[0])
+    own_up.start()
+    own_down = pltpu.make_async_copy(down_ref, wd.at[mine, :], w_sem.at[1])
+    own_down.start()
+
+    a = lax.broadcasted_iota(jnp.int32, (PAIRS, PAIRS), 0)
+    b = lax.broadcasted_iota(jnp.int32, (PAIRS, PAIRS), 1)
+    swap = (lax.rem(a, SUB) == lax.div(b, SUB)) & (lax.div(a, SUB) == lax.rem(b, SUB))
+    perm[...] = bf16(jnp.where(swap, 1.0, 0.0))
+    above[...] = bf16(jnp.where(a < b, 1.0, 0.0))
+
+    for copy in small:
+        copy.wait()
+    scale_vec[...] = jnp.zeros_like(scale_vec)
+    for k in range(slots):
+        live = jnp.where(count_ref[...] > k, 1.0, 0.0)
+        scale_vec[k : k + 1, :] = live * gates_ref[k : k + 1, :].astype(jnp.float32)
+        live3[0] = live
+    to_scalars = pltpu.make_async_copy(scale_vec, scale, s_sem)
+    to_scalars.start()
+
+    few = lax.broadcasted_iota(jnp.int32, (FEW, N), 0).astype(jnp.float32)
+
+    def squeeze(live):
+        position = dot(bf16(live), above[:N, :N])
+        return bf16(jnp.where((few == position) & (live > 0.5), 1.0, 0.0))
+
+    token = lax.broadcasted_iota(jnp.int32, (tok.shape[0], N), 0)
+    last_pick = jnp.where(token == pick_ref[slots - 1], 1.0, 0.0)
+    last_scaled = bf16(last_pick * scale_vec[slots - 1 : slots, :])
+    squeezed = squeeze(live3[0])
+    last_pick = bf16(dot(bf16(last_pick), squeezed, ((1,), (1,))))
+    last_scaled = bf16(dot(last_scaled, squeezed, ((1,), (1,))))
+    own_pick[...] = last_pick
+    for m in range(PLANE):
+        lanes = slice(m * LANES, (m + 1) * LANES)
+        third[m, :, :LANES] = bf16(dot(last_pick, tok_ref[:, lanes], ((0,), (0,))))
+        third[m, :, LANES:] = bf16(dot(last_scaled, grad_ref[:, lanes], ((0,), (0,))))
+
+    def by_row(g, carry):
+        r = pl.ds(pl.multiple_of(g * SUB, SUB), SUB)
+        both = jnp.concatenate(
+            [
+                jnp.concatenate([ref[r, f * LANES : (f + 1) * LANES] for f in range(SUB)], axis=0)
+                for ref in (tok_ref, grad_ref)
+            ],
+            axis=1,
+        )
+        out = bf16(dot(perm[...], both))
+        tok[r] = out[:, :LANES].reshape(SUB, SUB, LANES)
+        grad[r] = out[:, LANES:].reshape(SUB, SUB, LANES)
+        return carry
+
+    lax.fori_loop(0, tok.shape[0] // SUB, by_row, 0)
+    to_scalars.wait()
+
+    def ship(src, dst, target, send_sem, recv_sem):
+        pltpu.make_async_remote_copy(
+            src_ref=src, dst_ref=dst, send_sem=send_sem, recv_sem=recv_sem,
+            device_id={"expert": target}, device_id_type=MESH,
+        ).start()
+
+    def in_plane(src_of, dst, sem):
+        def one(k, carry):
+            peer = lax.rem(p + k, PLANE)
+            ship(src_of(peer), dst, z * PLANE + peer, t_send.at[sem], t_recv.at[sem])
+            return carry
+
+        pltpu.make_async_copy(src_of(p), dst, t_recv.at[sem]).start()
+        lax.fori_loop(1, PLANE, one, 0)
+
+    def along_z(src, dst, sems):
+        def one(k, carry):
+            zz = lax.rem(z + k, NZ)
+            ship(src.at[zz], dst.at[z], zz * PLANE + p, sems[0], sems[1])
+            return carry
+
+        pltpu.make_async_copy(src.at[z], dst.at[z], sems[1]).start()
+        lax.fori_loop(1, NZ, one, 0)
+
+    pl.semaphore_wait(barrier, N)
+
+    in_plane(lambda m: third.at[m], r1_in.at[p], 0)
+
+    def tell(k, carry):
+        ship(live3.at[0], meta1.at[p], z * PLANE + lax.rem(p + k, PLANE), m_send.at[0], m_recv.at[0])
+        return carry
+
+    pltpu.make_async_copy(live3.at[0], meta1.at[p], m_recv.at[0]).start()
+    lax.fori_loop(1, PLANE, tell, 0)
+
+    up_copy = pltpu.make_async_remote_copy(
+        src_ref=up_ref, dst_ref=wu.at[:, mine], send_sem=w_sem.at[2], recv_sem=w_sem.at[3],
+        device_id=partner, device_id_type=MESH,
+    )
+    up_copy.start()
+    down_copy = pltpu.make_async_remote_copy(
+        src_ref=down_ref, dst_ref=wd.at[mine, :], send_sem=w_sem.at[4], recv_sem=w_sem.at[5],
+        device_id=partner, device_id_type=MESH,
+    )
+    down_copy.start()
+
+    my_peer = (z * NY + y) * direct
+
+    def rows_at(c):
+        return pl.ds(c * quarter + my_peer, direct)
+
+    def fill(target):
+        for k in range(direct):
+            row = idx_ref[k, 0, target]
+            send[target, 0, k] = tok[row]
+            send[target, 1, k] = bf16(grad[row].astype(jnp.float32) * scale[k, target])
+
+    def push(n, carry):
+        c = lax.div(n, PEERS)
+        dz, dy = hop(lax.rem(n, PEERS))
+        target = expert_of(lax.rem(q_me + c, NX), lax.rem(z + dz, NZ), lax.rem(y + dy, NY))
+        fill(target)
+        ship(send.at[target], recv.at[:, rows_at(c)], target, f_send, f_recv.at[c * PARTS // NX])
+        return carry
+
+    def push_part(c):
+        lax.fori_loop(max(1, c * PEERS), (c + 1) * PEERS, push, 0)
+        if c == 0:
+            fill(me)
+            pltpu.make_async_copy(send.at[me], recv.at[:, rows_at(0)], f_recv.at[0]).start()
+
+    row_a = lax.broadcasted_iota(jnp.int32, (N, PAIRS), 0)
+    col_a = lax.broadcasted_iota(jnp.int32, (N, PAIRS), 1)
+    col_p = lax.broadcasted_iota(jnp.int32, (PLANE, PAIRS), 1)
+    row_p = lax.broadcasted_iota(jnp.int32, (PLANE, PAIRS), 0)
+    rank = lax.broadcasted_iota(jnp.int32, (CAP, PAIRS), 0).astype(jnp.float32)
+
+    def pack(zz, over):
+        pick_plane = jnp.where(row_a == zz * PLANE + lax.rem(col_a, PLANE), 1.0, 0.0)
+        spread = dot(meta1[...].reshape(PLANE, LANES), pick_plane)
+        own = jnp.where(lax.div(col_p, PLANE) == row_p, spread, 0.0)
+        live = jnp.sum(own, axis=0, keepdims=True)
+        position = dot(bf16(live), above[...])
+        chosen = bf16(jnp.where((rank == position) & (live > 0.5), 1.0, 0.0))
+        pack_out[zz] = chosen
+        meta2[zz, :, :PAIRS] = live
+        source = jnp.concatenate(
+            [r1[j, pl.ds(pl.multiple_of(zz * PLANE, PLANE), PLANE)] for j in range(PLANE)], axis=0
+        )
+        o2[zz] = bf16(dot(chosen, source))
+        return jnp.maximum(over, jnp.sum(live, axis=1, keepdims=True))
+
+    def send_thirds():
+        local_wait(meta1, m_recv.at[0])
+        local_wait(r1_in, t_recv.at[0])
+
+        def widen(j, crowd):
+            live = meta1[j]
+            chosen = squeeze(live)
+            pack_src[j] = chosen
+            r1[j] = bf16(dot(chosen, r1_in[j], ((0,), (0,))))
+            return jnp.maximum(crowd, jnp.sum(live, axis=1, keepdims=True))
+
+        crowd = lax.fori_loop(0, PLANE, widen, jnp.zeros((1, 1), jnp.float32))
+        most = lax.fori_loop(0, NZ, pack, jnp.zeros((1, 1), jnp.float32))
+        over = jnp.broadcast_to(jnp.where((most > CAP) | (crowd > FEW), 1.0, 0.0), (1, LANES))
+        for j in range(NZ):
+            meta2[j, :, PAIRS:] = over
+        along_z(meta2, got2, (m_send.at[1], m_recv.at[1]))
+        along_z(o2, r2, (t_send.at[1], t_recv.at[1]))
+
+    def compute(first, rows):
+        here = pl.ds(first, rows)
+        gate = jnp.zeros((rows, 1), jnp.float32)
+        for t in range(2 * half // 256):
+            cols = slice(t * 256, (t + 1) * 256)
+            hidden = dot(rows_x[here, :], wu[:, cols])
+            upstream = dot(rows_g[here, :], wd[cols, :], ((1,), (1,)))
+            s = jax.nn.sigmoid(hidden)
+            activation = bf16(hidden * s)
+            act[here, cols] = activation
+            dhid[here, cols] = bf16(upstream * (s * (1.0 + hidden * (1.0 - s))))
+            gate += jnp.sum(activation.astype(jnp.float32) * upstream, axis=1, keepdims=True)
+        return gate
+
+    def row_grads(first, rows, out):
+        for t in range(WIDE // 512):
+            cols = slice(t * 512, (t + 1) * 512)
+            out[:rows, cols] = bf16(dot(dhid[pl.ds(first, rows), :], wu[cols, :], ((1,), (1,))))
+
+    def peer_ids(c, sign, shape, axis):
+        row = lax.broadcasted_iota(jnp.int32, shape, axis) + c * per_chunk
+        turn = lax.div(row, quarter)
+        peer = lax.div(lax.rem(row, quarter), direct)
+        q = lax.rem(q_me + sign * turn + NX, NX)
+        return expert_of(q, lax.div(peer, NY), lax.rem(peer, NY)), lax.rem(row, direct)
+
+    groups = per_chunk // SUB
+    gsend[...] = jnp.zeros_like(gsend)
+
+    def chunk(c):
+        first = c * per_chunk
+        local_wait(recv.at[:, pl.ds(0, per_chunk)], f_recv.at[c])
+
+        def unpack(g, inner):
+            r = pl.ds(pl.multiple_of(first + g * SUB, SUB), SUB)
+            both = jnp.concatenate(
+                [recv[0, r].reshape(PAIRS, LANES), recv[1, r].reshape(PAIRS, LANES)], axis=1
+            )
+            out = bf16(dot(perm[...], both))
+            for f in range(SUB):
+                part = out[f * SUB : (f + 1) * SUB]
+                rows_x[r, f * LANES : (f + 1) * LANES] = part[:, :LANES]
+                rows_g[r, f * LANES : (f + 1) * LANES] = part[:, LANES:]
+            return inner
+
+        lax.fori_loop(0, groups, unpack, 0)
+        gate = compute(first, per_chunk)
+        row_grads(first, per_chunk, drow)
+
+        for g in range(0, groups, 2):
+            pair = [
+                jnp.concatenate(
+                    [
+                        drow[(g + h) * SUB : (g + h + 1) * SUB, f * LANES : (f + 1) * LANES]
+                        for f in range(SUB)
+                    ],
+                    axis=0,
+                )
+                for h in range(2)
+            ]
+            out = bf16(dot(perm[...], jnp.concatenate(pair, axis=1)))
+            for h in range(2):
+                r = pl.ds(first + (g + h) * SUB, SUB)
+                dsend[r] = out[:, h * LANES : (h + 1) * LANES].reshape(SUB, SUB, LANES)
+
+        if c == 0:
+            pltpu.make_async_copy(dsend.at[rows_at(0)], back.at[rows_at(0)], r_recv.at[0]).start()
+
+        def reply(n, inner):
+            turn = lax.div(n, PEERS)
+            dz, dy = hop(lax.rem(n, PEERS))
+            q = lax.rem(q_me - turn + NX, NX)
+            zz, yy = lax.rem(z - dz + NZ, NZ), lax.rem(y - dy + NY, NY)
+            source = pl.ds(turn * quarter + (zz * NY + yy) * direct, direct)
+            ship(
+                dsend.at[source], back.at[rows_at(turn)], expert_of(q, zz, yy),
+                r_send, r_recv.at[c],
+            )
+            return inner
+
+        span = N // PARTS
+        lax.fori_loop(max(1, c * span), (c + 1) * span, reply, 0)
+
+        owner, slot = peer_ids(c, -1, (1, per_chunk), 1)
+        to_source = jnp.where(
+            lax.broadcasted_iota(jnp.int32, (N, per_chunk), 0) == owner, 1.0, 0.0
+        )
+        _, slot = peer_ids(c, -1, (per_chunk, LANES), 0)
+        to_lane = lax.broadcasted_iota(jnp.int32, (per_chunk, LANES), 1) == slot
+        spread = lax.dot_general(
+            to_source, jnp.where(to_lane, gate, 0.0), (((1,), (0,)), ((), ())),
+            precision=lax.Precision.HIGHEST, preferred_element_type=jnp.float32,
+        )
+        gsend[...] += spread.reshape(N, 1, LANES)
+
+    def open_thirds():
+        local_wait(got2, m_recv.at[1])
+        local_wait(r2, t_recv.at[1])
+        flag = jnp.zeros((1, LANES), jnp.float32)
+        for j in range(NZ):
+            flag = jnp.maximum(flag, got2[j, :, PAIRS:])
+        flag_ref[...] = jnp.broadcast_to(flag, flag_ref.shape)
+
+        def one(zz, carry):
+            live = got2[zz][:, :PAIRS]
+            position = dot(bf16(live), above[...])
+            live = dot(bf16(live), perm[...])
+            position = dot(bf16(position), perm[...])
+            chosen = bf16(jnp.where((rank == position) & (live > 0.5), 1.0, 0.0))
+            pack_in[zz] = chosen
+            out = bf16(dot(chosen, r2[zz], ((0,), (0,))))
+            for j in range(PLANE):
+                o3[j, pl.ds(pl.multiple_of(zz * PLANE, PLANE), PLANE)] = out[j * SUB : (j + 1) * SUB]
+            return carry
+
+        lax.fori_loop(0, NZ, one, 0)
+        flags = got2[...].reshape(NZ, PAIRS + LANES)[:, :PAIRS]
+        row_s = lax.broadcasted_iota(jnp.int32, (PAIRS, N), 0)
+        col_s = lax.broadcasted_iota(jnp.int32, (PAIRS, N), 1)
+        row_z = lax.broadcasted_iota(jnp.int32, (NZ, N), 0)
+        col_z = lax.broadcasted_iota(jnp.int32, (NZ, N), 1)
+
+        def narrow(j, carry):
+            here = (lax.rem(row_s, PLANE) == j) & (lax.div(row_s, PLANE) == lax.rem(col_s, PLANE))
+            spread = dot(flags, jnp.where(here, 1.0, 0.0))
+            live = jnp.where(lax.div(col_z, PLANE) == row_z, spread, 0.0)
+            chosen = squeeze(jnp.sum(live, axis=0, keepdims=True))
+            pack_dst[j] = chosen
+            o3_out[j] = bf16(dot(chosen, o3[j]))
+            return carry
+
+        lax.fori_loop(0, PLANE, narrow, 0)
+        in_plane(lambda m: o3_out.at[m], r3.at[p], 2)
+
+    def run_thirds():
+        local_wait(r3, t_recv.at[2])
+        first = recv.shape[1]
+        for m in range(PLANE):
+            lanes = slice(m * LANES, (m + 1) * LANES)
+            rows_x[first:, lanes] = r3[m, :, :LANES]
+            rows_g[first:, lanes] = r3[m, :, LANES:]
+        gate = compute(first, FEW)
+        row_grads(first, FEW, d3)
+        in_plane(
+            lambda m: d3.at[:, pl.ds(pl.multiple_of(m * LANES, LANES), LANES)], rr1_in.at[p], 3
+        )
+        lane = lax.broadcasted_iota(jnp.int32, (FEW, LANES), 1)
+        spread = lax.dot_general(
+            pack_dst[p].astype(jnp.float32), jnp.where(lane == slots - 1, gate, 0.0),
+            (((0,), (0,)), ((), ())),
+            precision=lax.Precision.HIGHEST, preferred_element_type=jnp.float32,
+        )
+        gsend[...] += spread.reshape(N, 1, LANES)
+
+    def pack_back():
+        local_wait(rr1_in, t_recv.at[3])
+
+        def widen(j, carry):
+            rr1[j] = bf16(dot(pack_dst[j], rr1_in[j], ((0,), (0,))))
+            return carry
+
+        lax.fori_loop(0, PLANE, widen, 0)
+
+        def one(zz, carry):
+            source = jnp.concatenate(
+                [rr1[j, pl.ds(pl.multiple_of(zz * PLANE, PLANE), PLANE)] for j in range(PLANE)], axis=0
+            )
+            ro2[zz] = bf16(dot(pack_in[zz], source))
+            return carry
+
+        lax.fori_loop(0, NZ, one, 0)
+        along_z(ro2, rr2, (t_send.at[4], t_recv.at[4]))
+
+    def open_back():
+        local_wait(rr2, t_recv.at[4])
+
+        def one(zz, carry):
+            out = bf16(dot(pack_out[zz], rr2[zz], ((0,), (0,))))
+            for j in range(PLANE):
+                ro3[j, pl.ds(pl.multiple_of(zz * PLANE, PLANE), PLANE)] = out[j * SUB : (j + 1) * SUB]
+            return carry
+
+        lax.fori_loop(0, NZ, one, 0)
+
+        def narrow(j, carry):
+            ro3_out[j] = bf16(dot(pack_src[j], ro3[j]))
+            return carry
+
+        lax.fori_loop(0, PLANE, narrow, 0)
+        in_plane(lambda m: ro3_out.at[m], d3back.at[:, my_lanes], 5)
+
+    def weights_here():
+        own_up.wait()
+        own_down.wait()
+        up_copy.wait()
+        down_copy.wait()
+
+    tiles = WIDE // 512
+
+    def weight_grads():
+        pltpu.make_async_copy(gsend.at[me], gback.at[me], g_recv).start()
+
+        def reply_gate(n, carry):
+            target = lax.rem(me + n, N)
+            ship(gsend.at[target], gback.at[me], target, g_send, g_recv)
+            return carry
+
+        lax.fori_loop(1, N, reply_gate, 0)
+
+        flag_swap = pltpu.make_async_remote_copy(
+            src_ref=flag_ref, dst_ref=flag_in, send_sem=d_send.at[2], recv_sem=d_recv.at[2],
+            device_id=partner, device_id_type=MESH,
+        )
+        flag_swap.start()
+
+        first_core = core == 0
+        for t in range(tiles):
+            cols = slice(t * 512, (t + 1) * 512)
+            whole = dot(rows_x[:, cols], dhid[...], ((0,), (0,)))
+            left, right = whole[:, :half], whole[:, half:]
+            up_out[cols, :] = bf16(jnp.where(first_core, right, left))
+            up_own[cols, :] = jnp.where(first_core, left, right)
+        up_swap = pltpu.make_async_remote_copy(
+            src_ref=up_out, dst_ref=up_in, send_sem=d_send.at[0], recv_sem=d_recv.at[0],
+            device_id=partner, device_id_type=MESH,
+        )
+        up_swap.start()
+        for t in range(tiles):
+            cols = slice(t * 512, (t + 1) * 512)
+            whole = dot(act[...], rows_g[:, cols], ((0,), (0,)))
+            left, right = whole[:half], whole[half:]
+            down_out[:, cols] = bf16(jnp.where(first_core, right, left))
+            down_own[:, cols] = jnp.where(first_core, left, right)
+        down_swap = pltpu.make_async_remote_copy(
+            src_ref=down_out, dst_ref=down_in, send_sem=d_send.at[1], recv_sem=d_recv.at[1],
+            device_id=partner, device_id_type=MESH,
+        )
+        down_swap.start()
+        up_swap.wait()
+        for t in range(tiles):
+            cols = slice(t * 512, (t + 1) * 512)
+            dup_ref[cols, :] = bf16(up_own[cols, :] + up_in[cols, :].astype(jnp.float32))
+        down_swap.wait()
+        for t in range(tiles):
+            cols = slice(t * 512, (t + 1) * 512)
+            ddown_ref[:, cols] = bf16(down_own[:, cols] + down_in[:, cols].astype(jnp.float32))
+        flag_swap.wait()
+        flag_ref[...] = jnp.maximum(flag_ref[...], flag_in[...])
+
+    def finish_rows():
+        total[...] = jnp.zeros_like(total)
+
+        def combine(c, carry):
+            first = pl.multiple_of(c * per_chunk, SUB)
+            local_wait(back.at[pl.ds(0, per_chunk)], r_recv.at[c])
+            for g in range(0, groups, 2):
+                pair = [
+                    back[pl.ds(pl.multiple_of(first + (g + h) * SUB, SUB), SUB)].reshape(PAIRS, LANES)
+                    for h in range(2)
+                ]
+                out = bf16(dot(perm[...], jnp.concatenate(pair, axis=1)))
+                for h in range(2):
+                    for f in range(SUB):
+                        drow[(g + h) * SUB : (g + h + 1) * SUB, f * LANES : (f + 1) * LANES] = out[
+                            f * SUB : (f + 1) * SUB, h * LANES : (h + 1) * LANES
+                        ]
+            owner, slot = peer_ids(c, 1, (1, per_chunk), 1)
+            owned = jnp.where(
+                lax.broadcasted_iota(jnp.int32, (N, per_chunk), 0) == owner, 1.0, 0.0
+            )
+            picked = jnp.zeros((1, per_chunk), jnp.float32)
+            for k in range(direct):
+                picked += jnp.where(slot == k, dot(pick_ref[k].astype(jnp.float32), owned), 0.0)
+            rows = lax.broadcasted_iota(jnp.int32, (total.shape[0], per_chunk), 0)
+            chosen = bf16(jnp.where(rows.astype(jnp.float32) == picked, 1.0, 0.0))
+            for t in range(tiles):
+                cols = slice(t * 512, (t + 1) * 512)
+                total[:, cols] += dot(chosen, drow[:, cols])
+            return carry
+
+        lax.fori_loop(0, PARTS, combine, 0)
+        local_wait(d3back, t_recv.at[5])
+        for t in range(tiles):
+            cols = slice(t * 512, (t + 1) * 512)
+            dtok_ref[:, cols] = bf16(total[:, cols] + dot(own_pick[...], d3back[:, cols]))
+
+    push_part(0)
+    push_part(1)
+    send_thirds()
+    push_part(2)
+    push_part(3)
+    weights_here()
+    chunk(0)
+    open_thirds()
+    run_thirds()
+    chunk(1)
+    pack_back()
+    weight_grads()
+    open_back()
+    finish_rows()
+
+    local_wait(gback, g_recv)
+    eye = jnp.where(
+        lax.broadcasted_iota(jnp.int32, (8, LANES), 0)
+        == lax.broadcasted_iota(jnp.int32, (8, LANES), 1),
+        1.0,
+        0.0,
+    )
+    by_slot = lax.dot_general(
+        eye, gback[...].reshape(N, LANES), (((1,), (1,)), ((), ())),
+        precision=lax.Precision.HIGHEST, preferred_element_type=jnp.float32,
+    )
+    for k in range(slots):
+        c = scale_vec[k : k + 1, :]
+        inverse = jnp.where(c > 0.0, 1.0 / jnp.where(c > 0.0, c, 1.0), 0.0)
+        dgate_ref[k : k + 1, :] = bf16(by_slot[k : k + 1, :] * inverse)
+
+    local_wait(gsend.at[pl.ds(0, N - 1)], g_send)
+    local_wait(send.at[pl.ds(0, N - 1)], f_send)
+    local_wait(dsend.at[pl.ds(0, (N - 1) * direct)], r_send)
+    local_wait(meta1.at[pl.ds(0, PLANE - 1)], m_send.at[0])
+    local_wait(meta2.at[pl.ds(0, NZ - 1)], m_send.at[1])
+    for i, ref in enumerate((third, o2, o3_out, rr1_in, ro2, ro3_out)):
+        local_wait(ref.at[pl.ds(0, ref.shape[0] - 1)], t_send.at[i])
+
+
 def write_out(*refs):
     count = len(refs) // 2
     copies = [
@@ -374,54 +916,7 @@
 
     dma = pltpu.SemaphoreType.DMA
     outs = (((held, width), low), ((slots, experts), low), ((width, half), low), ((half, width), low))
-    results = pl.pallas_call(
-        kernel,
-        out_shape=tuple(pltpu.VMEM(shape, dtype) for shape, dtype in outs),
-        in_specs=[smem, hbm, hbm, hbm, vmem, vmem, hbm, hbm],
-        out_specs=(vmem, vmem, vmem, vmem),
-        scratch_shapes=[
-            pltpu.VMEM((slots, 1, experts), jnp.int32),
-            pltpu.VMEM((slots, experts), low),
-            pltpu.VMEM((1, experts), jnp.int32),
-            pltpu.VMEM((held, SUB, LANES), low),
-            pltpu.VMEM((held, SUB, LANES), low),
-            pltpu.VMEM((8, experts), full),
-            pltpu.SMEM((8, experts), full),
-            pltpu.VMEM((experts, 1, LANES), full),
-            pltpu.VMEM((experts, 2, slots, SUB, LANES), low),
-            pltpu.VMEM((2, total, SUB, LANES), low),
-            pltpu.VMEM((width, 2 * half), low),
-            pltpu.VMEM((2 * half, width), low),
-            pltpu.VMEM((total, width), low),
-            pltpu.VMEM((total, width), low),
-            pltpu.VMEM((total, 2 * half), low),
-            pltpu.VMEM((total, 2 * half), low),
-            pltpu.VMEM((PEERS * slots, width), low),
-            pltpu.VMEM((total, SUB, LANES), low),
-            pltpu.VMEM((total, SUB, LANES), low),
-            pltpu.VMEM((experts, 1, LANES), full),
-            pltpu.VMEM((width, half), full),
-            pltpu.VMEM((width, half), full),
-            pltpu.VMEM((half, width), full),
-            pltpu.VMEM((half, width), full),
-            pltpu.VMEM((held, width), full),
-            pltpu.VMEM((SUB * SUB, SUB * SUB), low),
-            dma((6,)),
-            dma,
-            dma((3,)),
-            dma,
-            dma((CHUNKS,)),
-            dma,
-            dma((CHUNKS,)),
-            dma,
-            dma,
-            dma((2,)),
-            dma((2,)),
-        ],
-        compiler_params=pltpu.CompilerParams(
-            collective_id=0, has_side_effects=True, vmem_limit_bytes=50 << 20
-        ),
-    )(
+    operands = (
         picks,
         stay(picks),
         stay(gates[0, 0].T),
@@ -431,14 +926,105 @@
         up_weight[0],
         down_weight[0],
     )
-    d_tokens, d_gate, d_up, d_down = pl.pallas_call(
-        write_out,
-        out_shape=tuple(jax.ShapeDtypeStruct(shape, dtype) for shape, dtype in outs),
-        in_specs=[vmem] * 4,
-        out_specs=(anywhere,) * 4,
-        scratch_shapes=[dma((4,))],
-        compiler_params=pltpu.CompilerParams(vmem_limit_bytes=1 << 20),
-    )(*(pltpu.with_memory_space_constraint(r, pltpu.VMEM) for r in results))
+    small = [
+        pltpu.VMEM((slots, 1, experts), jnp.int32),
+        pltpu.VMEM((slots, experts), low),
+        pltpu.VMEM((1, experts), jnp.int32),
+        pltpu.VMEM((held, SUB, LANES), low),
+        pltpu.VMEM((held, SUB, LANES), low),
+        pltpu.VMEM((8, experts), full),
+        pltpu.SMEM((8, experts), full),
+        pltpu.VMEM((experts, 1, LANES), full),
+    ]
+
+    def shared(sent, rows, parts, swapped):
+        return [
+            pltpu.VMEM((experts, 2, sent, SUB, LANES), low),
+            pltpu.VMEM((2, sent * experts, SUB, LANES), low),
+            pltpu.VMEM((width, 2 * half), low),
+            pltpu.VMEM((2 * half, width), low),
+            pltpu.VMEM((rows, width), low),
+            pltpu.VMEM((rows, width), low),
+            pltpu.VMEM((rows, 2 * half), low),
+            pltpu.VMEM((rows, 2 * half), low),
+            pltpu.VMEM((sent * experts // parts, width), low),
+            pltpu.VMEM((sent * experts, SUB, LANES), low),
+            pltpu.VMEM((sent * experts, SUB, LANES), low),
+            pltpu.VMEM((experts, 1, LANES), full),
+            *swapped,
+            pltpu.VMEM((held, width), full),
+            pltpu.VMEM((PAIRS, PAIRS), low),
+        ]
+
+    thirds = [
+        pltpu.VMEM((PAIRS, PAIRS), low),
+        pltpu.VMEM((PLANE, FEW, 2 * LANES), low),
+        pltpu.VMEM((PLANE, FEW, 2 * LANES), low),
+        pltpu.VMEM((PLANE, experts, 2 * LANES), low),
+        pltpu.VMEM((PLANE, 1, LANES), full),
+        pltpu.VMEM((1, 1, LANES), full),
+        pltpu.VMEM((NZ, CAP, 2 * LANES), low),
+        pltpu.VMEM((NZ, CAP, 2 * LANES), low),
+        pltpu.VMEM((NZ, 1, PAIRS + LANES), full),
+        pltpu.VMEM((NZ, 1, PAIRS + LANES), full),
+        pltpu.VMEM((PLANE, experts, 2 * LANES), low),
+        pltpu.VMEM((PLANE, FEW, 2 * LANES), low),
+        pltpu.VMEM((PLANE, FEW, 2 * LANES), low),
+        pltpu.VMEM((FEW, width), low),
+        pltpu.VMEM((PLANE, FEW, LANES), low),
+        pltpu.VMEM((PLANE, experts, LANES), low),
+        pltpu.VMEM((NZ, CAP, LANES), low),
+        pltpu.VMEM((NZ, CAP, LANES), low),
+        pltpu.VMEM((PLANE, experts, LANES), low),
+        pltpu.VMEM((PLANE, FEW, LANES), low),
+        pltpu.VMEM((FEW, width), low),
+        pltpu.VMEM((NZ, CAP, PAIRS), low),
+        pltpu.VMEM((NZ, CAP, PAIRS), low),
+        pltpu.VMEM((PLANE, FEW, experts), low),
+        pltpu.VMEM((PLANE, FEW, experts), low),
+        pltpu.VMEM((held, FEW), low),
+        pltpu.VMEM((8, LANES), full),
+    ]
+
+    def sems(chunks, swaps):
+        return [
+            dma((6,)), dma, dma((3,)), dma, dma((chunks,)), dma, dma((chunks,)),
+            dma, dma, dma((swaps,)), dma((swaps,)),
+        ]
+
+    def call(body, results, scratch, number):
+        return pl.pallas_call(
+            body,
+            out_shape=tuple(pltpu.VMEM(shape, dtype) for shape, dtype in results),
+            in_specs=[smem, hbm, hbm, hbm, vmem, vmem, hbm, hbm],
+            out_specs=(vmem,) * len(results),
+            scratch_shapes=scratch,
+            compiler_params=pltpu.CompilerParams(
+                collective_id=number, has_side_effects=True, vmem_limit_bytes=50 << 20
+            ),
+        )(*operands)
+
+    def store(*results):
+        return pl.pallas_call(
+            write_out,
+            out_shape=tuple(jax.ShapeDtypeStruct(shape, dtype) for shape, dtype in outs),
+            in_specs=[vmem] * 4,
+            out_specs=(anywhere,) * 4,
+            scratch_shapes=[dma((4,))],
+            compiler_params=pltpu.CompilerParams(vmem_limit_bytes=1 << 20),
+        )(*(pltpu.with_memory_space_constraint(r, pltpu.VMEM) for r in results))
+
+    *results, flag = call(
+        lean_kernel,
+        outs + (((8, LANES), full),),
+        small + shared(slots - 1, (slots - 1) * experts + FEW, PARTS, [pltpu.VMEM(shape, kind) for shape in ((width, half), (half, width)) for kind in (low, low, full)]) + thirds + sems(PARTS, 3) + [dma((6,)), dma((6,)), dma((2,)), dma((2,))],
+        0,
+    )
+
+    def padded(*unused):
+        return store(*call(padded_kernel, outs, small + shared(slots, total, CHUNKS, [pltpu.VMEM(shape, full) for shape in ((width, half), (half, width)) for _ in range(2)]) + sems(CHUNKS, 2), 1))
+
+    d_tokens, d_gate, d_up, d_down = lax.cond(flag[0, 0] > 0.5, padded, store, *results)
     return d_tokens[None], d_gate.T[None, None], d_up[None], d_down[None]
 
 

time: 123 us -> 113 us (0.919); the launches traced: 123 us -> 112 us
  Pallas kernels: 123 us -> 110 us
    pallas_call x2, Pallas kernels: 123 us -> 110 us  [the longest x1 108 us: call(): pl.pallas_call(body, out_shape=tuple((pltpu.VMEM(shape, dtype) for shape,...]
where the time goes in v5:
time: 113 us; the launch traced here: 112 us
  Pallas kernels  110 us (97%)
  between operations  1.52 us (1%)
    pallas_call x1, Pallas kernels, call(): pl.pallas_call(body, out_shape=tuple((pltpu.VMEM(shape, dtype) for shape,...  108 us

profile of v5, /device:TPU:32, one launch (start us, length us, event | category | flops | bytes accessed | tf_op | source)
XLA Modules:
  0.0 111.6 jit_solution(2785058082143183265)
XLA Ops:
  0.6 0.0 copy-start
  0.6 0.0 copy-start.1
  0.7 0.0 copy-start.2
  0.7 0.0 copy-start.3
  0.7 107.7 %shard_map.102 = (bf16[128,2048]{1,0:T(8,128)(2,1)S(1)}, bf16[3,128]{1,0:T(4,128)(2,1)S(1)}, bf16[2048,384]{1,0:T(8,128)(2,1)S(1)}, bf16[384,2048]{1,0:T(8,128)(2,1)S(1)}, f32[8,128]{1,0:T(8,128)S(1)}) custom-call(s32[3,1,128]{2,1,0:T(1,128)} %bitcast.26, s32[3,1,128]{2,1,0:T(1,128)} %bitcast.27, bf16[3,128]{1,0:T(4,128)(2,1)} %bitcast.29, ...), custom_call_target="tpu_custom_call" | custom-call | tf_op jit(solution)/shard_map/pallas_call | solution.py:996
  108.4 0.5 slice.3
  109.5 0.0 copy-done
  109.5 0.0 copy-done.1
  109.5 0.0 copy-done.2
  109.5 0.0 copy-done.3
  109.6 1.9 %conditional.1 = ((bf16[128,2048]{1,0:T(8,128)(2,1)}, bf16[3,128]{1,0:T(4,128)(2,1)}, bf16[2048,384]{1,0:T(8,128)(2,1)}, bf16[384,2048]{1,0:T(8,128)(2,1)})) conditional(s32[]{:T(128)} %bitcast.9, (bf16[128,2048]{1,0:T(8,128)(2,1)S(1)}, bf16[3,128]{1,0:T(4,128)(2,1)S(1)}, bf16[2048,384]{1,0:T(8,128)(2,1)S(1)}, ...), branch_computations={%region_0.0_spmd.clone, %region_1.0_spmd.clone} | conditional | bytes 8 | solution.py:1027
  109.6 1.9 %branch_0_fun.2 = (bf16[128,2048]{1,0:T(8,128)(2,1)}, bf16[3,128]{1,0:T(4,128)(2,1)}, bf16[2048,384]{1,0:T(8,128)(2,1)}, bf16[384,2048]{1,0:T(8,128)(2,1)}) custom-call(bf16[128,2048]{1,0:T(8,128)(2,1)S(1)} %get-tuple-element.95.refs_0_, bf16[3,128]{1,0:T(4,128)(2,1)S(1)} %get-tuple-element.96.refs_1_, bf16[2048,384]{1,0:T(8,128)(2,1)S(1)} %get-tuple-element.97.refs_2_, ...), custom_call_target="tpu_custom_call" | custom-call | tf_op jit(solution)/shard_map/cond/branch_0_fun/pallas_call | solution.py:1008
Async XLA Ops:
  0.6 108.9 %copy-start = (bf16[1,2048,384]{2,1,0:T(8,128)(2,1)S(1)}, bf16[1,2048,384]{2,1,0:T(8,128)(2,1)}, u32[]{:S(2)}) copy-start(bf16[1,2048,384]{2,1,0:T(8,128)(2,1)} %param.14) | copy-start | bytes 4718596
  0.6 108.9 %copy-start.1 = (bf16[1,384,2048]{2,1,0:T(8,128)(2,1)S(1)}, bf16[1,384,2048]{2,1,0:T(8,128)(2,1)}, u32[]{:S(2)}) copy-start(bf16[1,384,2048]{2,1,0:T(8,128)(2,1)} %param.15) | copy-start | bytes 4718596
  0.7 108.9 %copy-start.2 = (bf16[1,128,2048]{2,1,0:T(8,128)(2,1)S(1)}, bf16[1,128,2048]{2,1,0:T(8,128)(2,1)}, u32[]{:S(2)}) copy-start(bf16[1,128,2048]{2,1,0:T(8,128)(2,1)} %param.9) | copy-start | bytes 1572868
  0.7 108.9 %copy-start.3 = (bf16[1,128,2048]{2,1,0:T(8,128)(2,1)S(1)}, bf16[1,128,2048]{2,1,0:T(8,128)(2,1)}, u32[]{:S(2)}) copy-start(bf16[1,128,2048]{2,1,0:T(8,128)(2,1)} %param.10) | copy-start | bytes 1572868

commit v6 on v5

--- a/solution.py
+++ b/solution.py
@@ -401,8 +401,6 @@
 
     a = lax.broadcasted_iota(jnp.int32, (PAIRS, PAIRS), 0)
     b = lax.broadcasted_iota(jnp.int32, (PAIRS, PAIRS), 1)
-    swap = (lax.rem(a, SUB) == lax.div(b, SUB)) & (lax.div(a, SUB) == lax.rem(b, SUB))
-    perm[...] = bf16(jnp.where(swap, 1.0, 0.0))
     above[...] = bf16(jnp.where(a < b, 1.0, 0.0))
 
     for copy in small:
@@ -425,13 +423,66 @@
     last_pick = jnp.where(token == pick_ref[slots - 1], 1.0, 0.0)
     last_scaled = bf16(last_pick * scale_vec[slots - 1 : slots, :])
     squeezed = squeeze(live3[0])
-    last_pick = bf16(dot(bf16(last_pick), squeezed, ((1,), (1,))))
-    last_scaled = bf16(dot(last_scaled, squeezed, ((1,), (1,))))
-    own_pick[...] = last_pick
-    for m in range(PLANE):
-        lanes = slice(m * LANES, (m + 1) * LANES)
-        third[m, :, :LANES] = bf16(dot(last_pick, tok_ref[:, lanes], ((0,), (0,))))
-        third[m, :, LANES:] = bf16(dot(last_scaled, grad_ref[:, lanes], ((0,), (0,))))
+    own_pick[...] = bf16(dot(bf16(last_pick), squeezed, ((1,), (1,))))
+    chosen_rows = bf16(dot(squeezed, bf16(last_pick), ((1,), (1,))))
+    scaled_rows = bf16(dot(squeezed, last_scaled, ((1,), (1,))))
+    for t in range(WIDE // 512):
+        cols = slice(t * 512, (t + 1) * 512)
+        row_part = bf16(dot(chosen_rows, tok_ref[:, cols]))
+        grad_part = bf16(dot(scaled_rows, grad_ref[:, cols]))
+        for m in range(512 // LANES):
+            lanes = slice(m * LANES, (m + 1) * LANES)
+            third[t * 512 // LANES + m, :, :LANES] = row_part[:, lanes]
+            third[t * 512 // LANES + m, :, LANES:] = grad_part[:, lanes]
+
+    def ship(src, dst, target, send_sem, recv_sem):
+        pltpu.make_async_remote_copy(
+            src_ref=src, dst_ref=dst, send_sem=send_sem, recv_sem=recv_sem,
+            device_id={"expert": target}, device_id_type=MESH,
+        ).start()
+
+    def in_plane(src_of, dst, sem):
+        def one(k, carry):
+            peer = lax.rem(p + k, PLANE)
+            ship(src_of(peer), dst, z * PLANE + peer, t_send.at[sem], t_recv.at[sem])
+            return carry
+
+        pltpu.make_async_copy(src_of(p), dst, t_recv.at[sem]).start()
+        lax.fori_loop(1, PLANE, one, 0)
+
+    def along_z(src, dst, sems):
+        def one(k, carry):
+            zz = lax.rem(z + k, NZ)
+            ship(src.at[zz], dst.at[z], zz * PLANE + p, sems[0], sems[1])
+            return carry
+
+        pltpu.make_async_copy(src.at[z], dst.at[z], sems[1]).start()
+        lax.fori_loop(1, NZ, one, 0)
+
+    pl.semaphore_wait(barrier, N)
+
+    in_plane(lambda m: third.at[m], r1_in.at[p], 0)
+
+    def tell(k, carry):
+        ship(live3.at[0], meta1.at[p], z * PLANE + lax.rem(p + k, PLANE), m_send.at[0], m_recv.at[0])
+        return carry
+
+    pltpu.make_async_copy(live3.at[0], meta1.at[p], m_recv.at[0]).start()
+    lax.fori_loop(1, PLANE, tell, 0)
+
+    up_copy = pltpu.make_async_remote_copy(
+        src_ref=up_ref, dst_ref=wu.at[:, mine], send_sem=w_sem.at[2], recv_sem=w_sem.at[3],
+        device_id=partner, device_id_type=MESH,
+    )
+    up_copy.start()
+    down_copy = pltpu.make_async_remote_copy(
+        src_ref=down_ref, dst_ref=wd.at[mine, :], send_sem=w_sem.at[4], recv_sem=w_sem.at[5],
+        device_id=partner, device_id_type=MESH,
+    )
+    down_copy.start()
+
+    swap = (lax.rem(a, SUB) == lax.div(b, SUB)) & (lax.div(a, SUB) == lax.rem(b, SUB))
+    perm[...] = bf16(jnp.where(swap, 1.0, 0.0))
 
     def by_row(g, carry):
         r = pl.ds(pl.multiple_of(g * SUB, SUB), SUB)
@@ -449,52 +500,6 @@
 
     lax.fori_loop(0, tok.shape[0] // SUB, by_row, 0)
     to_scalars.wait()
-
-    def ship(src, dst, target, send_sem, recv_sem):
-        pltpu.make_async_remote_copy(
-            src_ref=src, dst_ref=dst, send_sem=send_sem, recv_sem=recv_sem,
-            device_id={"expert": target}, device_id_type=MESH,
-        ).start()
-
-    def in_plane(src_of, dst, sem):
-        def one(k, carry):
-            peer = lax.rem(p + k, PLANE)
-            ship(src_of(peer), dst, z * PLANE + peer, t_send.at[sem], t_recv.at[sem])
-            return carry
-
-        pltpu.make_async_copy(src_of(p), dst, t_recv.at[sem]).start()
-        lax.fori_loop(1, PLANE, one, 0)
-
-    def along_z(src, dst, sems):
-        def one(k, carry):
-            zz = lax.rem(z + k, NZ)
-            ship(src.at[zz], dst.at[z], zz * PLANE + p, sems[0], sems[1])
-            return carry
-
-        pltpu.make_async_copy(src.at[z], dst.at[z], sems[1]).start()
-        lax.fori_loop(1, NZ, one, 0)
-
-    pl.semaphore_wait(barrier, N)
-
-    in_plane(lambda m: third.at[m], r1_in.at[p], 0)
-
-    def tell(k, carry):
-        ship(live3.at[0], meta1.at[p], z * PLANE + lax.rem(p + k, PLANE), m_send.at[0], m_recv.at[0])
-        return carry
-
-    pltpu.make_async_copy(live3.at[0], meta1.at[p], m_recv.at[0]).start()
-    lax.fori_loop(1, PLANE, tell, 0)
-
-    up_copy = pltpu.make_async_remote_copy(
-        src_ref=up_ref, dst_ref=wu.at[:, mine], send_sem=w_sem.at[2], recv_sem=w_sem.at[3],
-        device_id=partner, device_id_type=MESH,
-    )
-    up_copy.start()
-    down_copy = pltpu.make_async_remote_copy(
-        src_ref=down_ref, dst_ref=wd.at[mine, :], send_sem=w_sem.at[4], recv_sem=w_sem.at[5],
-        device_id=partner, device_id_type=MESH,
-    )
-    down_copy.start()
 
     my_peer = (z * NY + y) * direct
 

time: 113 us -> 115 us (1.018)
  Pallas kernels: 110 us -> 112 us
    pallas_call x1, Pallas kernels: 108 us -> 110 us  [call(): pl.pallas_call(body, out_shape=tuple((pltpu.VMEM(shape, dtype) for shape,...]
where the time goes in v6:
time: 115 us; the launch traced here: 114 us
  Pallas kernels  112 us (97%)
  between operations  1.52 us (1%)
    pallas_call x1, Pallas kernels, call(): pl.pallas_call(body, out_shape=tuple((pltpu.VMEM(shape, dtype) for shape,...  110 us

profile of v6, /device:TPU:32, one launch (start us, length us, event | category | flops | bytes accessed | tf_op | source)
XLA Modules:
  0.0 114.0 jit_solution(8510701209318591342)
XLA Ops:
  0.6 0.0 copy-start
  0.6 0.0 copy-start.1
  0.7 0.0 copy-start.2
  0.7 0.0 copy-start.3
  0.7 110.0 %shard_map.102 = (bf16[128,2048]{1,0:T(8,128)(2,1)S(1)}, bf16[3,128]{1,0:T(4,128)(2,1)S(1)}, bf16[2048,384]{1,0:T(8,128)(2,1)S(1)}, bf16[384,2048]{1,0:T(8,128)(2,1)S(1)}, f32[8,128]{1,0:T(8,128)S(1)}) custom-call(s32[3,1,128]{2,1,0:T(1,128)} %bitcast.26, s32[3,1,128]{2,1,0:T(1,128)} %bitcast.27, bf16[3,128]{1,0:T(4,128)(2,1)} %bitcast.29, ...), custom_call_target="tpu_custom_call" | custom-call | tf_op jit(solution)/shard_map/pallas_call | solution.py:1001
  110.7 0.5 slice.3
  111.9 0.0 copy-done
  111.9 0.0 copy-done.1
  111.9 0.0 copy-done.2
  111.9 0.0 copy-done.3
  111.9 1.9 %conditional.1 = ((bf16[128,2048]{1,0:T(8,128)(2,1)}, bf16[3,128]{1,0:T(4,128)(2,1)}, bf16[2048,384]{1,0:T(8,128)(2,1)}, bf16[384,2048]{1,0:T(8,128)(2,1)})) conditional(s32[]{:T(128)} %bitcast.9, (bf16[128,2048]{1,0:T(8,128)(2,1)S(1)}, bf16[3,128]{1,0:T(4,128)(2,1)S(1)}, bf16[2048,384]{1,0:T(8,128)(2,1)S(1)}, ...), branch_computations={%region_0.0_spmd.clone, %region_1.0_spmd.clone} | conditional | bytes 8 | solution.py:1032
  111.9 1.9 %branch_0_fun.2 = (bf16[128,2048]{1,0:T(8,128)(2,1)}, bf16[3,128]{1,0:T(4,128)(2,1)}, bf16[2048,384]{1,0:T(8,128)(2,1)}, bf16[384,2048]{1,0:T(8,128)(2,1)}) custom-call(bf16[128,2048]{1,0:T(8,128)(2,1)S(1)} %get-tuple-element.95.refs_0_, bf16[3,128]{1,0:T(4,128)(2,1)S(1)} %get-tuple-element.96.refs_1_, bf16[2048,384]{1,0:T(8,128)(2,1)S(1)} %get-tuple-element.97.refs_2_, ...), custom_call_target="tpu_custom_call" | custom-call | tf_op jit(solution)/shard_map/cond/branch_0_fun/pallas_call | solution.py:1013
Async XLA Ops:
  0.6 111.2 %copy-start = (bf16[1,2048,384]{2,1,0:T(8,128)(2,1)S(1)}, bf16[1,2048,384]{2,1,0:T(8,128)(2,1)}, u32[]{:S(2)}) copy-start(bf16[1,2048,384]{2,1,0:T(8,128)(2,1)} %param.14) | copy-start | bytes 4718596
  0.6 111.2 %copy-start.1 = (bf16[1,384,2048]{2,1,0:T(8,128)(2,1)S(1)}, bf16[1,384,2048]{2,1,0:T(8,128)(2,1)}, u32[]{:S(2)}) copy-start(bf16[1,384,2048]{2,1,0:T(8,128)(2,1)} %param.15) | copy-start | bytes 4718596
  0.7 111.2 %copy-start.2 = (bf16[1,128,2048]{2,1,0:T(8,128)(2,1)S(1)}, bf16[1,128,2048]{2,1,0:T(8,128)(2,1)}, u32[]{:S(2)}) copy-start(bf16[1,128,2048]{2,1,0:T(8,128)(2,1)} %param.9) | copy-start | bytes 1572868
  0.7 111.2 %copy-start.3 = (bf16[1,128,2048]{2,1,0:T(8,128)(2,1)S(1)}, bf16[1,128,2048]{2,1,0:T(8,128)(2,1)}, u32[]{:S(2)}) copy-start(bf16[1,128,2048]{2,1,0:T(8,128)(2,1)} %param.10) | copy-start | bytes 1572868

commit v7 on v5

--- a/solution.py
+++ b/solution.py
@@ -352,12 +352,12 @@
 
 def lean_kernel(
     idx_ref, pick_hbm, gates_hbm, count_hbm, tok_ref, grad_ref, up_ref, down_ref,
-    dtok_ref, dgate_ref, dup_ref, ddown_ref, flag_ref,
+    dtok_ref, dgate_ref, dup_ref, ddown_ref, over_ref,
     pick_ref, gates_ref, count_ref, tok, grad, scale_vec, scale, gback,
     send, recv, wu, wd, rows_x, rows_g, act, dhid, drow, dsend, back, gsend,
     up_out, up_in, up_own, down_out, down_in, down_own, total, perm, above,
     third, r1_in, r1, meta1, live3, o2, r2, meta2, got2, o3, o3_out, r3,
-    d3, rr1_in, rr1, ro2, rr2, ro3, ro3_out, d3back, pack_out, pack_in, pack_src, pack_dst, own_pick, flag_in,
+    d3, rr1_in, rr1, ro2, rr2, ro3, ro3_out, d3back, pack_out, pack_in, pack_src, pack_dst, own_pick, flag_ref, flag_in,
     w_sem, s_sem, small_sem, f_send, f_recv, r_send, r_recv, g_send, g_recv, d_send, d_recv,
     t_send, t_recv, m_send, m_recv,
 ):
@@ -425,13 +425,17 @@
     last_pick = jnp.where(token == pick_ref[slots - 1], 1.0, 0.0)
     last_scaled = bf16(last_pick * scale_vec[slots - 1 : slots, :])
     squeezed = squeeze(live3[0])
-    last_pick = bf16(dot(bf16(last_pick), squeezed, ((1,), (1,))))
-    last_scaled = bf16(dot(last_scaled, squeezed, ((1,), (1,))))
-    own_pick[...] = last_pick
-    for m in range(PLANE):
-        lanes = slice(m * LANES, (m + 1) * LANES)
-        third[m, :, :LANES] = bf16(dot(last_pick, tok_ref[:, lanes], ((0,), (0,))))
-        third[m, :, LANES:] = bf16(dot(last_scaled, grad_ref[:, lanes], ((0,), (0,))))
+    own_pick[...] = bf16(dot(bf16(last_pick), squeezed, ((1,), (1,))))
+    chosen_rows = bf16(dot(squeezed, bf16(last_pick), ((1,), (1,))))
+    scaled_rows = bf16(dot(squeezed, last_scaled, ((1,), (1,))))
+    for t in range(WIDE // 512):
+        cols = slice(t * 512, (t + 1) * 512)
+        row_part = bf16(dot(chosen_rows, tok_ref[:, cols]))
+        grad_part = bf16(dot(scaled_rows, grad_ref[:, cols]))
+        for m in range(512 // LANES):
+            lanes = slice(m * LANES, (m + 1) * LANES)
+            third[t * 512 // LANES + m, :, :LANES] = row_part[:, lanes]
+            third[t * 512 // LANES + m, :, LANES:] = grad_part[:, lanes]
 
     def by_row(g, carry):
         r = pl.ds(pl.multiple_of(g * SUB, SUB), SUB)
@@ -474,28 +478,6 @@
         pltpu.make_async_copy(src.at[z], dst.at[z], sems[1]).start()
         lax.fori_loop(1, NZ, one, 0)
 
-    pl.semaphore_wait(barrier, N)
-
-    in_plane(lambda m: third.at[m], r1_in.at[p], 0)
-
-    def tell(k, carry):
-        ship(live3.at[0], meta1.at[p], z * PLANE + lax.rem(p + k, PLANE), m_send.at[0], m_recv.at[0])
-        return carry
-
-    pltpu.make_async_copy(live3.at[0], meta1.at[p], m_recv.at[0]).start()
-    lax.fori_loop(1, PLANE, tell, 0)
-
-    up_copy = pltpu.make_async_remote_copy(
-        src_ref=up_ref, dst_ref=wu.at[:, mine], send_sem=w_sem.at[2], recv_sem=w_sem.at[3],
-        device_id=partner, device_id_type=MESH,
-    )
-    up_copy.start()
-    down_copy = pltpu.make_async_remote_copy(
-        src_ref=down_ref, dst_ref=wd.at[mine, :], send_sem=w_sem.at[4], recv_sem=w_sem.at[5],
-        device_id=partner, device_id_type=MESH,
-    )
-    down_copy.start()
-
     my_peer = (z * NY + y) * direct
 
     def rows_at(c):
@@ -507,19 +489,50 @@
             send[target, 0, k] = tok[row]
             send[target, 1, k] = bf16(grad[row].astype(jnp.float32) * scale[k, target])
 
-    def push(n, carry):
-        c = lax.div(n, PEERS)
-        dz, dy = hop(lax.rem(n, PEERS))
-        target = expert_of(lax.rem(q_me + c, NX), lax.rem(z + dz, NZ), lax.rem(y + dy, NY))
-        fill(target)
-        ship(send.at[target], recv.at[:, rows_at(c)], target, f_send, f_recv.at[c * PARTS // NX])
+    def target_of(c, i):
+        dz, dy = hop(i)
+        return expert_of(lax.rem(q_me + c, NX), lax.rem(z + dz, NZ), lax.rem(y + dy, NY))
+
+    def fill_first(i, carry):
+        fill(target_of(0, i))
         return carry
 
     def push_part(c):
-        lax.fori_loop(max(1, c * PEERS), (c + 1) * PEERS, push, 0)
+        def push(i, carry):
+            target = target_of(c, i)
+            if c > 0:
+                fill(target)
+            ship(send.at[target], recv.at[:, rows_at(c)], target, f_send, f_recv.at[c * PARTS // NX])
+            return carry
+
         if c == 0:
-            fill(me)
             pltpu.make_async_copy(send.at[me], recv.at[:, rows_at(0)], f_recv.at[0]).start()
+        lax.fori_loop(1 if c == 0 else 0, PEERS, push, 0)
+
+    lax.fori_loop(0, PEERS, fill_first, 0)
+    pl.semaphore_wait(barrier, N)
+
+    push_part(0)
+
+    in_plane(lambda m: third.at[m], r1_in.at[p], 0)
+
+    def tell(k, carry):
+        ship(live3.at[0], meta1.at[p], z * PLANE + lax.rem(p + k, PLANE), m_send.at[0], m_recv.at[0])
+        return carry
+
+    pltpu.make_async_copy(live3.at[0], meta1.at[p], m_recv.at[0]).start()
+    lax.fori_loop(1, PLANE, tell, 0)
+
+    up_copy = pltpu.make_async_remote_copy(
+        src_ref=up_ref, dst_ref=wu.at[:, mine], send_sem=w_sem.at[2], recv_sem=w_sem.at[3],
+        device_id=partner, device_id_type=MESH,
+    )
+    up_copy.start()
+    down_copy = pltpu.make_async_remote_copy(
+        src_ref=down_ref, dst_ref=wd.at[mine, :], send_sem=w_sem.at[4], recv_sem=w_sem.at[5],
+        device_id=partner, device_id_type=MESH,
+    )
+    down_copy.start()
 
     row_a = lax.broadcasted_iota(jnp.int32, (N, PAIRS), 0)
     col_a = lax.broadcasted_iota(jnp.int32, (N, PAIRS), 1)
@@ -808,7 +821,7 @@
             cols = slice(t * 512, (t + 1) * 512)
             ddown_ref[:, cols] = bf16(down_own[:, cols] + down_in[:, cols].astype(jnp.float32))
         flag_swap.wait()
-        flag_ref[...] = jnp.maximum(flag_ref[...], flag_in[...])
+        over_ref[0, 0] = jnp.max(jnp.maximum(flag_ref[...], flag_in[...]))
 
     def finish_rows():
         total[...] = jnp.zeros_like(total)
@@ -847,7 +860,6 @@
             cols = slice(t * 512, (t + 1) * 512)
             dtok_ref[:, cols] = bf16(total[:, cols] + dot(own_pick[...], d3back[:, cols]))
 
-    push_part(0)
     push_part(1)
     send_thirds()
     push_part(2)
@@ -916,6 +928,7 @@
 
     dma = pltpu.SemaphoreType.DMA
     outs = (((held, width), low), ((slots, experts), low), ((width, half), low), ((half, width), low))
+    kept = tuple(pltpu.VMEM(shape, dtype) for shape, dtype in outs)
     operands = (
         picks,
         stay(picks),
@@ -984,6 +997,7 @@
         pltpu.VMEM((PLANE, FEW, experts), low),
         pltpu.VMEM((held, FEW), low),
         pltpu.VMEM((8, LANES), full),
+        pltpu.VMEM((8, LANES), full),
     ]
 
     def sems(chunks, swaps):
@@ -995,9 +1009,9 @@
     def call(body, results, scratch, number):
         return pl.pallas_call(
             body,
-            out_shape=tuple(pltpu.VMEM(shape, dtype) for shape, dtype in results),
+            out_shape=tuple(results),
             in_specs=[smem, hbm, hbm, hbm, vmem, vmem, hbm, hbm],
-            out_specs=(vmem,) * len(results),
+            out_specs=(vmem,) * 4 + (smem,) * (len(results) - 4),
             scratch_shapes=scratch,
             compiler_params=pltpu.CompilerParams(
                 collective_id=number, has_side_effects=True, vmem_limit_bytes=50 << 20
@@ -1016,13 +1030,13 @@
 
     *results, flag = call(
         lean_kernel,
-        outs + (((8, LANES), full),),
+        kept + (jax.ShapeDtypeStruct((1, 1), full),),
         small + shared(slots - 1, (slots - 1) * experts + FEW, PARTS, [pltpu.VMEM(shape, kind) for shape in ((width, half), (half, width)) for kind in (low, low, full)]) + thirds + sems(PARTS, 3) + [dma((6,)), dma((6,)), dma((2,)), dma((2,))],
         0,
     )
 
     def padded(*unused):
-        return store(*call(padded_kernel, outs, small + shared(slots, total, CHUNKS, [pltpu.VMEM(shape, full) for shape in ((width, half), (half, width)) for _ in range(2)]) + sems(CHUNKS, 2), 1))
+        return store(*call(padded_kernel, kept, small + shared(slots, total, CHUNKS, [pltpu.VMEM(shape, full) for shape in ((width, half), (half, width)) for _ in range(2)]) + sems(CHUNKS, 2), 1))
 
     d_tokens, d_gate, d_up, d_down = lax.cond(flag[0, 0] > 0.5, padded, store, *results)
     return d_tokens[None], d_gate.T[None, None], d_up[None], d_down[None]

time: 113 us -> 113 us (level)
  no operation moved by 1% of the time
where the time goes in v7:
time: 113 us; the launch traced here: 111 us
  Pallas kernels  110 us (97%)
  between operations  1.49 us (1%)
    pallas_call x1, Pallas kernels, call(): pl.pallas_call(body, out_shape=tuple(results), in_specs=[smem, hbm, hbm,...  108 us

profile of v7, /device:TPU:32, one launch (start us, length us, event | category | flops | bytes accessed | tf_op | source)
XLA Modules:
  0.0 111.2 jit_solution(2026722076778602345)
XLA Ops:
  0.6 0.0 copy-start
  0.6 0.0 copy-start.1
  0.7 0.0 copy-start.2
  0.7 0.0 copy-start.3
  0.7 107.8 %shard_map.102 = (bf16[128,2048]{1,0:T(8,128)(2,1)S(1)}, bf16[3,128]{1,0:T(4,128)(2,1)S(1)}, bf16[2048,384]{1,0:T(8,128)(2,1)S(1)}, bf16[384,2048]{1,0:T(8,128)(2,1)S(1)}, f32[1,1]{1,0:T(1,128)}) custom-call(s32[3,1,128]{2,1,0:T(1,128)} %bitcast.26, s32[3,1,128]{2,1,0:T(1,128)} %bitcast.27, bf16[3,128]{1,0:T(4,128)(2,1)} %bitcast.29, s32[1,128]{1,0:T(1,128)} %bitcast.31, ...), custom_call_target="tpu_custom_call" | custom-call | tf_op jit(solution)/shard_map/pallas_call | solution.py:1010
  109.1 0.0 copy-done
  109.1 0.0 copy-done.1
  109.1 0.0 copy-done.2
  109.1 0.0 copy-done.3
  109.1 1.9 %conditional.1 = ((bf16[128,2048]{1,0:T(8,128)(2,1)}, bf16[3,128]{1,0:T(4,128)(2,1)}, bf16[2048,384]{1,0:T(8,128)(2,1)}, bf16[384,2048]{1,0:T(8,128)(2,1)})) conditional(s32[]{:T(128)} %bitcast.9, (bf16[128,2048]{1,0:T(8,128)(2,1)S(1)}, bf16[3,128]{1,0:T(4,128)(2,1)S(1)}, bf16[2048,384]{1,0:T(8,128)(2,1)S(1)}, ...), branch_computations={%region_0.0_spmd.clone, %region_1.0_spmd.clone} | conditional | bytes 8 | solution.py:1041
  109.1 1.9 %branch_0_fun.2 = (bf16[128,2048]{1,0:T(8,128)(2,1)}, bf16[3,128]{1,0:T(4,128)(2,1)}, bf16[2048,384]{1,0:T(8,128)(2,1)}, bf16[384,2048]{1,0:T(8,128)(2,1)}) custom-call(bf16[128,2048]{1,0:T(8,128)(2,1)S(1)} %get-tuple-element.95.refs_0_, bf16[3,128]{1,0:T(4,128)(2,1)S(1)} %get-tuple-element.96.refs_1_, bf16[2048,384]{1,0:T(8,128)(2,1)S(1)} %get-tuple-element.97.refs_2_, ...), custom_call_target="tpu_custom_call" | custom-call | tf_op jit(solution)/shard_map/cond/branch_0_fun/pallas_call | solution.py:1022
Async XLA Ops:
  0.6 108.5 %copy-start = (bf16[1,2048,384]{2,1,0:T(8,128)(2,1)S(1)}, bf16[1,2048,384]{2,1,0:T(8,128)(2,1)}, u32[]{:S(2)}) copy-start(bf16[1,2048,384]{2,1,0:T(8,128)(2,1)} %param.14) | copy-start | bytes 4718596
  0.6 108.5 %copy-start.1 = (bf16[1,384,2048]{2,1,0:T(8,128)(2,1)S(1)}, bf16[1,384,2048]{2,1,0:T(8,128)(2,1)}, u32[]{:S(2)}) copy-start(bf16[1,384,2048]{2,1,0:T(8,128)(2,1)} %param.15) | copy-start | bytes 4718596
  0.7 108.5 %copy-start.2 = (bf16[1,128,2048]{2,1,0:T(8,128)(2,1)S(1)}, bf16[1,128,2048]{2,1,0:T(8,128)(2,1)}, u32[]{:S(2)}) copy-start(bf16[1,128,2048]{2,1,0:T(8,128)(2,1)} %param.9) | copy-start | bytes 1572868
  0.7 108.5 %copy-start.3 = (bf16[1,128,2048]{2,1,0:T(8,128)(2,1)S(1)}, bf16[1,128,2048]{2,1,0:T(8,128)(2,1)}, u32[]{:S(2)}) copy-start(bf16[1,128,2048]{2,1,0:T(8,128)(2,1)} %param.10) | copy-start | bytes 1572868

commit v8 on v7

--- a/solution.py
+++ b/solution.py
@@ -773,6 +773,19 @@
 
     tiles = WIDE // 512
 
+    flag_swap = pltpu.make_async_remote_copy(
+        src_ref=flag_ref, dst_ref=flag_in, send_sem=d_send.at[2], recv_sem=d_recv.at[2],
+        device_id=partner, device_id_type=MESH,
+    )
+    up_swap = pltpu.make_async_remote_copy(
+        src_ref=up_out, dst_ref=up_in, send_sem=d_send.at[0], recv_sem=d_recv.at[0],
+        device_id=partner, device_id_type=MESH,
+    )
+    down_swap = pltpu.make_async_remote_copy(
+        src_ref=down_out, dst_ref=down_in, send_sem=d_send.at[1], recv_sem=d_recv.at[1],
+        device_id=partner, device_id_type=MESH,
+    )
+
     def weight_grads():
         pltpu.make_async_copy(gsend.at[me], gback.at[me], g_recv).start()
 
@@ -783,10 +796,6 @@
 
         lax.fori_loop(1, N, reply_gate, 0)
 
-        flag_swap = pltpu.make_async_remote_copy(
-            src_ref=flag_ref, dst_ref=flag_in, send_sem=d_send.at[2], recv_sem=d_recv.at[2],
-            device_id=partner, device_id_type=MESH,
-        )
         flag_swap.start()
 
         first_core = core == 0
@@ -796,10 +805,6 @@
             left, right = whole[:, :half], whole[:, half:]
             up_out[cols, :] = bf16(jnp.where(first_core, right, left))
             up_own[cols, :] = jnp.where(first_core, left, right)
-        up_swap = pltpu.make_async_remote_copy(
-            src_ref=up_out, dst_ref=up_in, send_sem=d_send.at[0], recv_sem=d_recv.at[0],
-            device_id=partner, device_id_type=MESH,
-        )
         up_swap.start()
         for t in range(tiles):
             cols = slice(t * 512, (t + 1) * 512)
@@ -807,11 +812,9 @@
             left, right = whole[:half], whole[half:]
             down_out[:, cols] = bf16(jnp.where(first_core, right, left))
             down_own[:, cols] = jnp.where(first_core, left, right)
-        down_swap = pltpu.make_async_remote_copy(
-            src_ref=down_out, dst_ref=down_in, send_sem=d_send.at[1], recv_sem=d_recv.at[1],
-            device_id=partner, device_id_type=MESH,
-        )
         down_swap.start()
+
+    def finish_grads():
         up_swap.wait()
         for t in range(tiles):
             cols = slice(t * 512, (t + 1) * 512)
@@ -872,6 +875,7 @@
     pack_back()
     weight_grads()
     open_back()
+    finish_grads()
     finish_rows()
 
     local_wait(gback, g_recv)

time: 113 us -> 113 us (level)
  no operation moved by 1% of the time
where the time goes in v8:
time: 113 us; the launch traced here: 111 us
  Pallas kernels  110 us (97%)
  between operations  1.49 us (1%)
    pallas_call x1, Pallas kernels, call(): pl.pallas_call(body, out_shape=tuple(results), in_specs=[smem, hbm, hbm,...  108 us

profile of v8, /device:TPU:32, one launch (start us, length us, event | category | flops | bytes accessed | tf_op | source)
XLA Modules:
  0.0 111.2 jit_solution(2550037347284703507)
XLA Ops:
  0.6 0.0 copy-start
  0.6 0.0 copy-start.1
  0.7 0.0 copy-start.2
  0.7 0.0 copy-start.3
  0.7 107.8 %shard_map.102 = (bf16[128,2048]{1,0:T(8,128)(2,1)S(1)}, bf16[3,128]{1,0:T(4,128)(2,1)S(1)}, bf16[2048,384]{1,0:T(8,128)(2,1)S(1)}, bf16[384,2048]{1,0:T(8,128)(2,1)S(1)}, f32[1,1]{1,0:T(1,128)}) custom-call(s32[3,1,128]{2,1,0:T(1,128)} %bitcast.26, s32[3,1,128]{2,1,0:T(1,128)} %bitcast.27, bf16[3,128]{1,0:T(4,128)(2,1)} %bitcast.29, s32[1,128]{1,0:T(1,128)} %bitcast.31, ...), custom_call_target="tpu_custom_call" | custom-call | tf_op jit(solution)/shard_map/pallas_call | solution.py:1014
  109.1 0.0 copy-done
  109.1 0.0 copy-done.1
  109.1 0.0 copy-done.2
  109.1 0.0 copy-done.3
  109.1 1.9 %conditional.1 = ((bf16[128,2048]{1,0:T(8,128)(2,1)}, bf16[3,128]{1,0:T(4,128)(2,1)}, bf16[2048,384]{1,0:T(8,128)(2,1)}, bf16[384,2048]{1,0:T(8,128)(2,1)})) conditional(s32[]{:T(128)} %bitcast.9, (bf16[128,2048]{1,0:T(8,128)(2,1)S(1)}, bf16[3,128]{1,0:T(4,128)(2,1)S(1)}, bf16[2048,384]{1,0:T(8,128)(2,1)S(1)}, ...), branch_computations={%region_0.0_spmd.clone, %region_1.0_spmd.clone} | conditional | bytes 8 | solution.py:1045
  109.1 1.9 %branch_0_fun.2 = (bf16[128,2048]{1,0:T(8,128)(2,1)}, bf16[3,128]{1,0:T(4,128)(2,1)}, bf16[2048,384]{1,0:T(8,128)(2,1)}, bf16[384,2048]{1,0:T(8,128)(2,1)}) custom-call(bf16[128,2048]{1,0:T(8,128)(2,1)S(1)} %get-tuple-element.95.refs_0_, bf16[3,128]{1,0:T(4,128)(2,1)S(1)} %get-tuple-element.96.refs_1_, bf16[2048,384]{1,0:T(8,128)(2,1)S(1)} %get-tuple-element.97.refs_2_, ...), custom_call_target="tpu_custom_call" | custom-call | tf_op jit(solution)/shard_map/cond/branch_0_fun/pallas_call | solution.py:1026
Async XLA Ops:
  0.6 108.5 %copy-start = (bf16[1,2048,384]{2,1,0:T(8,128)(2,1)S(1)}, bf16[1,2048,384]{2,1,0:T(8,128)(2,1)}, u32[]{:S(2)}) copy-start(bf16[1,2048,384]{2,1,0:T(8,128)(2,1)} %param.14) | copy-start | bytes 4718596
  0.6 108.5 %copy-start.1 = (bf16[1,384,2048]{2,1,0:T(8,128)(2,1)S(1)}, bf16[1,384,2048]{2,1,0:T(8,128)(2,1)}, u32[]{:S(2)}) copy-start(bf16[1,384,2048]{2,1,0:T(8,128)(2,1)} %param.15) | copy-start | bytes 4718596
  0.7 108.5 %copy-start.2 = (bf16[1,128,2048]{2,1,0:T(8,128)(2,1)S(1)}, bf16[1,128,2048]{2,1,0:T(8,128)(2,1)}, u32[]{:S(2)}) copy-start(bf16[1,128,2048]{2,1,0:T(8,128)(2,1)} %param.9) | copy-start | bytes 1572868
  0.7 108.5 %copy-start.3 = (bf16[1,128,2048]{2,1,0:T(8,128)(2,1)S(1)}, bf16[1,128,2048]{2,1,0:T(8,128)(2,1)}, u32[]{:S(2)}) copy-start(bf16[1,128,2048]{2,1,0:T(8,128)(2,1)} %param.10) | copy-start | bytes 1572868
